TPU v7x, 32 devices: a whole 2x2x4 slice. The times are simulated.
32 devices in a mesh: ctx: 4 (over x, core), head: 8 (over z, y).
Axes of the slice: x: 2, y: 2, z: 4, core: 2. Of those that a mesh axis runs over, the one named last changes fastest.
Arguments:
- tokens: bfloat16 [1024, 8192], P('ctx', 'head'), may hold values from -6 to 6
- out_grad: bfloat16 [1024, 8192], P('ctx', 'head'), may hold values from -6 to 6
- w_query: bfloat16 [8192, 4096], P(None, 'head'), may hold values from -0.0625 to 0.0625
- w_key: bfloat16 [8192, 4096], P(None, 'head'), may hold values from -0.0625 to 0.0625
- w_value: bfloat16 [8192, 4096], P(None, 'head'), may hold values from -0.0625 to 0.0625
- w_output: bfloat16 [8192, 4096], P(None, 'head'), may hold values from -0.09375 to 0.09375
Outputs:
- input_grad: bfloat16 [1024, 8192], P('ctx', 'head')
- grad_query: bfloat16 [8192, 4096], P('ctx', 'head')
- grad_key: bfloat16 [8192, 4096], P('ctx', 'head')
- grad_value: bfloat16 [8192, 4096], P('ctx', 'head')
- grad_output: bfloat16 [8192, 4096], P('ctx', 'head')
All inputs are finite; a program needn't handle non-finite values.
Results may differ from a plain program's by a relative error of at most 0.017.
Values may be sent and summed in bfloat16 or wider, within the bound.
No kernel may reach another device: no remote copies, remote signals or barrier semaphores. Data moves between devices by JAX's collectives and lax.ppermute only.
A program may use at most 256 MiB of HBM per device.

v0:
```python
import jax
import jax.numpy as jnp
from jax import lax
from jax.sharding import PartitionSpec as P

HD = 128


def carried_in(x, axis, combine, identity, reverse):
    count, here = (lax.axis_size(axis), lax.axis_index(axis))
    everything = lax.all_gather(x.astype(jnp.bfloat16), axis)
    start = jnp.broadcast_to(jnp.asarray(identity, x.dtype), x.shape)

    def lap(k, before):
        at = count - 1 - k if reverse else k
        reached = at > here if reverse else at < here
        new = combine(before, everything[at].astype(x.dtype))
        return jnp.where(reached, new, before)

    return lax.fori_loop(0, count, lap, start)


def feature(values):
    return jnp.where(values > 0, values + 1.0, jnp.exp(jnp.minimum(values, 0.0)))


def slope(values):
    return jnp.where(values > 0, 1.0, jnp.exp(jnp.minimum(values, 0.0)))


def split_heads(values, number):
    return values.reshape(values.shape[0], number, HD).transpose(1, 0, 2)


def merge_heads(values):
    return values.transpose(1, 0, 2).reshape(values.shape[1], -1)


def add_states(earlier, later):
    return earlier + later


def local(tokens, out_grad, w_query, w_key, w_value, w_output):
    highest = lax.Precision.HIGHEST
    whole_tokens, whole_grads = (
        lax.all_gather(tokens, "head", axis=1, tiled=True),
        lax.all_gather(out_grad, "head", axis=1, tiled=True),
    )
    length = tokens.shape[0]
    number = w_query.shape[1] // HD
    query_lin = jnp.dot(whole_tokens, w_query, preferred_element_type=jnp.float32)
    key_lin = jnp.dot(whole_tokens, w_key, preferred_element_type=jnp.float32)
    query_feat = split_heads(feature(query_lin).astype(jnp.bfloat16), number)
    key_feat = split_heads(feature(key_lin).astype(jnp.bfloat16), number)
    value_lin = jnp.dot(whole_tokens, w_value, preferred_element_type=jnp.float32)
    value_feat = split_heads(value_lin.astype(jnp.bfloat16), number)
    causal = lax.broadcasted_iota(jnp.int32, (length, length), 0) >= lax.broadcasted_iota(
        jnp.int32, (length, length), 1
    )
    raw_scores = jnp.einsum(
        "htd,hsd->hts", query_feat, key_feat, preferred_element_type=jnp.float32
    )
    scores = jnp.where(causal, raw_scores, 0.0).astype(jnp.bfloat16)
    local_kv = jnp.einsum("htd,hte->hde", key_feat, value_feat, preferred_element_type=jnp.float32)
    prefix = carried_in(local_kv, "ctx", add_states, jnp.zeros_like(local_kv), False)
    attended = jnp.einsum("hts,hse->hte", scores, value_feat, preferred_element_type=jnp.float32)
    attended = attended + jnp.einsum(
        "htd,hde->hte", query_feat.astype(jnp.float32), prefix, precision=highest
    )
    scale = lax.rsqrt(jnp.mean(attended * attended, axis=-1, keepdims=True) + 1e-06)
    normed = attended * scale
    attn_rows = merge_heads(normed).astype(jnp.bfloat16)
    attn_grad = split_heads(
        jnp.dot(whole_grads, w_output, preferred_element_type=jnp.float32), number
    )
    out_delta = (
        scale * (attn_grad - normed * jnp.mean(attn_grad * normed, axis=-1, keepdims=True))
    ).astype(jnp.bfloat16)
    local_qg = jnp.einsum("htd,hte->hde", query_feat, out_delta, preferred_element_type=jnp.float32)
    suffix = carried_in(local_qg, "ctx", add_states, jnp.zeros_like(local_qg), True)
    raw_grad = jnp.einsum("hte,hse->hts", out_delta, value_feat, preferred_element_type=jnp.float32)
    score_grad = jnp.where(causal, raw_grad, 0.0).astype(jnp.bfloat16)
    delta_wide = out_delta.astype(jnp.float32)
    feat_q = jnp.einsum("hts,hsd->htd", score_grad, key_feat, preferred_element_type=jnp.float32)
    feat_q = feat_q + jnp.einsum("hte,hde->htd", delta_wide, prefix, precision=highest)
    feat_k = jnp.einsum("hts,htd->hsd", score_grad, query_feat, preferred_element_type=jnp.float32)
    feat_k = feat_k + jnp.einsum(
        "hse,hde->hsd", value_feat.astype(jnp.float32), suffix, precision=highest
    )
    feat_v = jnp.einsum("hts,hte->hse", scores, out_delta, preferred_element_type=jnp.float32)
    feat_v = feat_v + jnp.einsum(
        "hsd,hde->hse", key_feat.astype(jnp.float32), suffix, precision=highest
    )
    query_pre = (merge_heads(feat_q) * slope(query_lin)).astype(jnp.bfloat16)
    key_pre = (merge_heads(feat_k) * slope(key_lin)).astype(jnp.bfloat16)
    value_pre = merge_heads(feat_v).astype(jnp.bfloat16)
    partial_value = jnp.einsum("ti,di->td", query_pre, w_query, preferred_element_type=jnp.float32)
    partial_value = partial_value + jnp.einsum(
        "ti,di->td", key_pre, w_key, preferred_element_type=jnp.float32
    )
    partial_value = partial_value + jnp.einsum(
        "ti,di->td", value_pre, w_value, preferred_element_type=jnp.float32
    )
    input_grad = lax.psum_scatter(
        partial_value.astype(jnp.bfloat16), "head", scatter_dimension=1, tiled=True
    )
    columns = query_pre.shape[1]
    sums = lax.psum_scatter(
        jnp.concatenate(
            [
                jnp.einsum(
                    "td,ti->di", whole_tokens, query_pre, preferred_element_type=jnp.float32
                ),
                jnp.einsum("td,ti->di", whole_tokens, key_pre, preferred_element_type=jnp.float32),
                jnp.einsum(
                    "td,ti->di", whole_tokens, value_pre, preferred_element_type=jnp.float32
                ),
                jnp.einsum("td,ti->di", whole_grads, attn_rows, preferred_element_type=jnp.float32),
            ],
            axis=1,
        ).astype(jnp.bfloat16),
        "ctx",
        scatter_dimension=0,
        tiled=True,
    ).astype(jnp.float32)
    grad_query = sums[:, 0:columns].astype(jnp.bfloat16)
    grad_key = sums[:, columns : 2 * columns].astype(jnp.bfloat16)
    grad_value = sums[:, 2 * columns : 3 * columns].astype(jnp.bfloat16)
    grad_output = sums[:, 3 * columns : 4 * columns].astype(jnp.bfloat16)
    return (input_grad, grad_query, grad_key, grad_value, grad_output)


def solution(mesh):
    placed = (
        P("ctx", "head"),
        P("ctx", "head"),
        P(None, "head"),
        P(None, "head"),
        P(None, "head"),
        P(None, "head"),
    )
    return jax.shard_map(
        local,
        mesh=mesh,
        in_specs=placed,
        out_specs=(
            P("ctx", "head"),
            P("ctx", "head"),
            P("ctx", "head"),
            P("ctx", "head"),
            P("ctx", "head"),
        ),
        check_vma=False,
    )
```

profile of v0, /device:TPU:0, one launch (start us, length us, event | category | flops | bytes accessed | tf_op | source)
XLA Modules:
  0.0 562.7 jit_solution(1147776180573535859)
XLA Ops:
  8.8 77.5 %all-gather.5.cloned.1.call-done = bf16[256,8192]{1,0:T(8,128)(2,1)} async-done(((bf16[256,1024]{1,0:T(8,128)(2,1)}), bf16[256,8192]{1,0:T(8,128)(2,1)}) %all-gather.5.cloned.1.call-update) | async-done | bytes 4194320 | tf_op jit(solution)/shard_map/all_gather | solution.py:46
  86.3 7.8 %select_convert_fusion.1 = (bf16[256,512]{1,0:T(8,128)(2,1)S(1)}, f32[256,512]{1,0:T(8,128)}) fusion(bf16[256,8192]{1,0:T(8,128)(2,1)} %all-gather.5.cloned.1.call-done, bf16[8192,512]{1,0:T(8,128)(2,1)} %param.12), kind=kOutput, calls=%fused_computation.36 | convolution fusion | flops 2148139008 | bytes 13369344 | tf_op jit(solution)/shard_map/dot_general | solution.py:51
  94.2 7.3 %fusion.23 = f32[256,512]{1,0:T(8,128)S(1)} fusion(bf16[256,8192]{1,0:T(8,128)(2,1)} %all-gather.5.cloned.1.call-done, bf16[8192,512]{1,0:T(8,128)(2,1)} %param.13), kind=kOutput, calls=%fused_computation.58 | convolution fusion | flops 2147483648 | bytes 13107200 | tf_op jit(solution)/shard_map/dot_general | solution.py:52
  101.7 5.7 %fusion.8 = bf16[32,4,8,128]{3,2,1,0:T(8,128)(2,1)S(1)} fusion(bf16[256,8192]{1,0:T(8,128)(2,1)S(1)} %copy-done, bf16[8192,512]{1,0:T(8,128)(2,1)} %param.14), kind=kOutput, calls=%fused_computation.24 | convolution fusion | flops 2147614720 | bytes 12845056 | tf_op jit(solution)/shard_map/dot_general | solution.py:55
  107.8 7.2 %all-gather = bf16[16,128,128]{2,1,0:T(8,128)(2,1)S(1)} all-gather(bf16[4,128,128]{2,1,0:T(8,128)(2,1)S(1)} %convolution_convert_fusion.6), channel_id=2, replica_groups=mesh['ctx'=4,'head'=8] {'ctx'}, dimensions={0}, use_global_device_ids=true | all-gather | bytes 655360 | tf_op jit(solution)/shard_map/all_gather | solution.py:11
  116.7 43.5 %all-gather.7.cloned.1.call-done = bf16[256,8192]{1,0:T(8,128)(2,1)} async-done(((bf16[256,1024]{1,0:T(8,128)(2,1)}), bf16[256,8192]{1,0:T(8,128)(2,1)}) %all-gather.7.cloned.1.call-update) | async-done | bytes 4194320 | tf_op jit(solution)/shard_map/all_gather | solution.py:47
  160.2 8.0 %multiply_reduce_fusion = (f32[4,256]{1,0:T(4,128)S(1)}, f32[256,512]{0,1:T(8,128)S(1)}) fusion(f32[4,256,128]{1,2,0:T(8,128)S(1)} %get-tuple-element.261, f32[4,256]{1,0:T(4,128)S(1)} %get-tuple-element.257, bf16[256,8192]{1,0:T(8,128)(2,1)} %all-gather.7.cloned.1.call-done, bf16[8192,512]{1,0:T(8,128)(2,1)} %param.15), kind=kOutput, calls=%fused_computation.32 | convolution fusion | flops 2147875840 | bytes 13639680 | tf_op jit(solution)/shard_map/dot_general | solution.py:74
  171.1 7.3 %all-gather.1 = bf16[16,128,128]{2,1,0:T(8,128)(2,1)S(1)} all-gather(bf16[4,128,128]{2,1,0:T(8,128)(2,1)S(1)} %convolution_convert_fusion.5), channel_id=3, replica_groups=mesh['ctx'=4,'head'=8] {'ctx'}, dimensions={0}, use_global_device_ids=true | all-gather | bytes 655360 | tf_op jit(solution)/shard_map/all_gather | solution.py:11
  180.6 1.6 fusion.7
  183.5 7.7 %fusion.3 = bf16[8192,512]{0,1:T(8,128)(2,1)} fusion(bf16[256,512]{0,1:T(8,128)(2,1)S(1)} %bitcast.126, bf16[256,8192]{1,0:T(8,128)(2,1)} %all-gather.7.cloned.1.call-done), kind=kOutput, calls=%fused_computation.10 | convolution fusion | flops 2151677952 | bytes 12845056 | tf_op jit(solution)/shard_map/td,ti->di/dot_general | solution.py:118
  191.2 5.6 fusion.2
  196.8 5.6 fusion.1
  202.3 5.6 fusion
  207.9 22.8 %pad_maximum_fusion = bf16[8192,2048]{0,1:T(8,128)(2,1)} fusion(bf16[8192,512]{0,1:T(8,128)(2,1)} %fusion.3, bf16[8192,512]{0,1:T(8,128)(2,1)} %fusion.2, bf16[8192,512]{0,1:T(8,128)(2,1)} %fusion.1, bf16[8192,512]{0,1:T(8,128)(2,1)} %fusion), kind=kLoop, calls=%fused_computation.2 | loop fusion | flops 134217728 | bytes 67108864 | tf_op jit(solution)/shard_map/concatenate | solution.py:109
  231.0 5.8 %fusion.24 = f32[256,8192]{1,0:T(8,128)S(1)} fusion(bf16[256,512]{1,0:T(8,128)(2,1)S(1)} %multiply_convert_fusion.1, bf16[8192,512]{1,0:T(8,128)(2,1)} %param.12), kind=kOutput, calls=%fused_computation.59 | convolution fusion | flops 2147483648 | bytes 17039360 | tf_op jit(solution)/shard_map/ti,di->td/dot_general | solution.py:97
  236.8 12.6 %convolution_add_fusion.1 = f32[256,8192]{1,0:T(8,128)} fusion(f32[256,8192]{1,0:T(8,128)S(1)} %fusion.24, bf16[256,512]{1,0:T(8,128)(2,1)S(1)} %multiply_convert_fusion, bf16[8192,512]{1,0:T(8,128)(2,1)} %param.13), kind=kOutput, calls=%fused_computation.12 | convolution fusion | flops 2149580800 | bytes 25427968 | tf_op jit(solution)/shard_map/ti,di->td/dot_general | solution.py:98
  249.4 14.6 %fusion.4 = bf16[256,8192]{1,0:T(8,128)(2,1)} fusion(f32[256,8192]{1,0:T(8,128)} %convolution_add_fusion.1, bf16[256,512]{0,1:T(8,128)(2,1)S(1)} %bitcast.123, bf16[8192,512]{1,0:T(8,128)(2,1)} %param.14), kind=kOutput, calls=%fused_computation.13 | convolution fusion | flops 2151677952 | bytes 21233664 | tf_op jit(solution)/shard_map/ti,di->td/dot_general | solution.py:101
  264.1 199.8 %reduce-scatter.5.cloned.1.call-done = bf16[2048,2048]{0,1:T(8,128)(2,1)} async-done(((bf16[8192,2048]{0,1:T(8,128)(2,1)}), bf16[2048,2048]{0,1:T(8,128)(2,1)}) %reduce-scatter.5.cloned.1.call-update) | async-done | bytes 8388624 | tf_op jit(solution)/shard_map/reduce_scatter | solution.py:108
  463.8 5.6 fusion.22
  469.4 3.9 copy.47
  473.3 3.9 copy.48
  477.2 3.9 copy.49
  481.2 2.5 copy.50
  483.7 72.6 %reduce-scatter.3.cloned.1.call-done = bf16[256,1024]{1,0:T(8,128)(2,1)} async-done(((bf16[256,8192]{1,0:T(8,128)(2,1)}), bf16[256,1024]{1,0:T(8,128)(2,1)}) %reduce-scatter.3.cloned.1.call-update) | async-done | bytes 524304 | tf_op jit(solution)/shard_map/reduce_scatter | solution.py:104
  (48 shorter events, 11.1 us)
Async XLA Ops:
  7.2 79.1 %all-gather.5.cloned.1.call-start = ((), (), s32[]{:S(2)}) async-start(), calls=%async_computation.2 | async-start | bytes 4718592 | tf_op jit(solution)/shard_map/all_gather | solution.py:46
  7.9 152.3 %all-gather.7.cloned.1.call-start = ((), (), s32[]{:S(2)}) async-start(), calls=%async_computation.3 | async-start | bytes 4718592 | tf_op jit(solution)/shard_map/all_gather | solution.py:47
  8.6 455.2 %reduce-scatter.5.cloned.1.call-start = ((), (), s32[]{:S(2)}) async-start(), calls=%async_computation.5 | async-start | bytes 41943040 | tf_op jit(solution)/shard_map/reduce_scatter | solution.py:108
  94.2 7.5 %copy-start = (bf16[256,8192]{1,0:T(8,128)(2,1)S(1)}, bf16[256,8192]{1,0:T(8,128)(2,1)}, u32[]{:S(2)}) copy-start(bf16[256,8192]{1,0:T(8,128)(2,1)} %all-gather.5.cloned.1.call-done) | copy-start | bytes 12582916
  107.5 60.8 %copy-start.2 = (bf16[32,4,8,128]{3,2,1,0:T(8,128)(2,1)}, bf16[32,4,8,128]{3,2,1,0:T(8,128)(2,1)S(1)}, u32[]{:S(2)}) copy-start(bf16[32,4,8,128]{3,2,1,0:T(8,128)(2,1)S(1)} %fusion.8) | copy-start | bytes 786436
  180.6 10.6 %copy-start.1 = (bf16[256,8192]{1,0:T(8,128)(2,1)S(1)}, bf16[256,8192]{1,0:T(8,128)(2,1)}, u32[]{:S(2)}) copy-start(bf16[256,8192]{1,0:T(8,128)(2,1)} %all-gather.5.cloned.1.call-done) | copy-start | bytes 12582916
  230.7 325.5 %reduce-scatter.3.cloned.1.call-start = ((), (), s32[]{:S(2)}) async-start(), calls=%async_computation.4 | async-start | bytes 4718592 | tf_op jit(solution)/shard_map/reduce_scatter | solution.py:104
Sparse Core Ops, SparseCore 0:
  10.2 76.0 all-gather.4
  88.5 71.6 all-gather.6
  230.9 232.9 reduce-scatter.4
  467.9 88.2 reduce-scatter.2
where the time goes:
time: 563 us
  waiting for transfers between devices  395 us (70%)
  matrix products  93.2 us (17%)
  other arithmetic  25.3 us (4%)
  local copies, waits for them, and re-layouts  20.4 us (4%)
  blocking collectives  14.6 us (3%)
  between operations  14 us (2%)
    reduce_scatter x1, waiting for transfers between devices, local(): lax.psum_scatter(jnp.concatenate([jnp.einsum('td,ti->di', whole_tokens, q...  200 us
    all_gather x1, waiting for transfers between devices, local(): lax.all_gather(tokens, 'head', axis=1, tiled=True)  77.5 us
    reduce_scatter x1, waiting for transfers between devices, local(): lax.psum_scatter(partial_value.astype(jnp.bfloat16), 'head', scatter_dime...  72.6 us
    all_gather x1, waiting for transfers between devices, local(): lax.all_gather(out_grad, 'head', axis=1, tiled=True)  43.5 us
    concatenate x1, other arithmetic, local(): jnp.concatenate([jnp.einsum('td,ti->di', whole_tokens, query_pre, preferr...  22.8 us
    dot_general x1, matrix products, local(): jnp.einsum('ti,di->td', value_pre, w_value, preferred_element_type=jnp.fl...  14.6 us
    all_gather x2, blocking collectives, carried_in(): everything = lax.all_gather(x.astype(jnp.bfloat16), axis)  14.6 us
    unnamed x10, local copies, waits for them, and re-layouts  14.3 us
  transfers between devices with their start and end apart: 4, of which 4 were waited for; matrix products, arithmetic and copies ran while one was open for 13% of the time, Pallas kernels for 0%

commit v1 on v0

v1 whole, which is shorter than its diff:
```python
import jax
import jax.numpy as jnp
from jax import lax
from jax.sharding import PartitionSpec as P

HD = 128
F32 = jnp.float32
BF16 = jnp.bfloat16


def feature(values):
    return jnp.where(values > 0, values + 1.0, jnp.exp(jnp.minimum(values, 0.0)))


def slope(values):
    return jnp.where(values > 0, 1.0, jnp.exp(jnp.minimum(values, 0.0)))


def split_heads(values, number):
    return values.reshape(values.shape[0], number, HD).transpose(1, 0, 2)


def merge_heads(values):
    return values.transpose(1, 0, 2).reshape(values.shape[1], -1)


def ein(spec, left, right):
    return jnp.einsum(spec, left, right, preferred_element_type=F32)


class Lines:
    def __init__(self):
        self.nh = lax.axis_size("head")
        self.nc = lax.axis_size("ctx")
        self.Z = 4 if self.nh % 4 == 0 else 1
        self.Y = self.nh // self.Z
        here = lax.axis_index("head")
        self.c = lax.axis_index("ctx")
        self.z = here // self.Y
        self.y = here % self.Y

    def along_z(self, x):
        return lax.ppermute(x, "head", [(i, (i + self.Y) % self.nh) for i in range(self.nh)])

    def along_y(self, x):
        Y = self.Y
        return lax.ppermute(x, "head", [(i, i // Y * Y + (i + 1) % Y) for i in range(self.nh)])

    def across(self, x, j):
        return lax.ppermute(x, "ctx", [(i, i ^ j) for i in range(self.nc)])

    def shard(self, k, j):
        return ((self.z - k) % self.Z) * self.Y + (self.y - j) % self.Y


def gather_features(at, x):
    rows, cols = x.shape
    parts = []
    now = x
    for k in range(at.Z):
        if k:
            now = at.along_z(now)
        side = now
        for j in range(at.Y):
            if j:
                side = at.along_y(side)
            parts.append((at.shard(k, j), side))
    whole = jnp.zeros((rows, cols * at.nh), x.dtype)
    for place, part in parts:
        whole = lax.dynamic_update_slice(whole, part, (0, place * cols))
    return whole


def by_slices(at, whole):
    width = whole.shape[1] // at.nc
    out = []
    for j in range(at.nc):
        piece = lax.dynamic_slice_in_dim(whole, (at.c ^ j) * width, width, 1)
        out.append(at.across(piece, j) if j else piece)
    return jnp.concatenate(out, axis=0)


def by_blocks(at, x):
    return jnp.concatenate([at.across(x, j) if j else x for j in range(at.nc)], axis=0)


def states(at, x, later):
    every = lax.all_gather(x.astype(BF16), "ctx").astype(F32)
    index = jnp.arange(at.nc)
    keep = (index > at.c) if later else (index < at.c)
    return jnp.sum(jnp.where(keep[:, None, None, None], every, 0.0), axis=0)


def local(tokens, out_grad, w_query, w_key, w_value, w_output):
    at = Lines()
    length, cols = tokens.shape
    number = w_query.shape[1] // HD
    whole_tokens = gather_features(at, tokens)
    whole_grads = gather_features(at, out_grad)
    query_lin = jnp.dot(whole_tokens, w_query, preferred_element_type=F32)
    key_lin = jnp.dot(whole_tokens, w_key, preferred_element_type=F32)
    value_lin = jnp.dot(whole_tokens, w_value, preferred_element_type=F32)
    token_slices = by_slices(at, whole_tokens)
    grad_slices = by_slices(at, whole_grads)
    query_feat = split_heads(feature(query_lin).astype(BF16), number)
    key_feat = split_heads(feature(key_lin).astype(BF16), number)
    value_feat = split_heads(value_lin.astype(BF16), number)
    causal = lax.broadcasted_iota(jnp.int32, (length, length), 0) >= lax.broadcasted_iota(
        jnp.int32, (length, length), 1
    )
    scores = jnp.where(causal, ein("htd,hsd->hts", query_feat, key_feat), 0.0).astype(BF16)
    local_kv = ein("htd,hte->hde", key_feat, value_feat)
    prefix = states(at, local_kv, False).astype(BF16)
    attended = ein("hts,hse->hte", scores, value_feat) + ein("htd,hde->hte", query_feat, prefix)
    scale = lax.rsqrt(jnp.mean(attended * attended, axis=-1, keepdims=True) + 1e-06)
    normed = attended * scale
    attn_rows = merge_heads(normed).astype(BF16)
    rows_all = by_blocks(at, attn_rows)
    attn_grad = split_heads(jnp.dot(whole_grads, w_output, preferred_element_type=F32), number)
    out_delta = (
        scale * (attn_grad - normed * jnp.mean(attn_grad * normed, axis=-1, keepdims=True))
    ).astype(BF16)
    local_qg = ein("htd,hte->hde", query_feat, out_delta)
    suffix = states(at, local_qg, True).astype(BF16)
    score_grad = jnp.where(causal, ein("hte,hse->hts", out_delta, value_feat), 0.0).astype(BF16)
    feat_q = ein("hts,hsd->htd", score_grad, key_feat) + ein("hte,hde->htd", out_delta, prefix)
    feat_k = ein("hts,htd->hsd", score_grad, query_feat) + ein("hse,hde->hsd", value_feat, suffix)
    feat_v = ein("hts,hte->hse", scores, out_delta) + ein("hsd,hde->hse", key_feat, suffix)
    query_pre = (merge_heads(feat_q) * slope(query_lin)).astype(BF16)
    key_pre = (merge_heads(feat_k) * slope(key_lin)).astype(BF16)
    value_pre = merge_heads(feat_v).astype(BF16)
    pre = jnp.concatenate([query_pre, key_pre, value_pre], axis=1)

    def part(place):
        def term(left, w):
            rows = lax.dynamic_slice_in_dim(w, place * cols, cols, 0)
            return ein("ti,di->td", left, rows)

        return term(query_pre, w_query) + term(key_pre, w_key) + term(value_pre, w_value)

    total = None
    for k in range(1, at.Z + 1):
        held = None
        for j in range(1, at.Y + 1):
            mine = part(at.shard(k, j))
            held = mine if held is None else mine + held.astype(F32)
            if j < at.Y:
                held = at.along_y(held.astype(BF16))
        total = held if total is None else held + total.astype(F32)
        if k < at.Z:
            total = at.along_z(total.astype(BF16))
    input_grad = total.astype(BF16)
    pre_all = by_blocks(at, pre)
    width = query_pre.shape[1]
    weight_grads = ein("td,ti->di", token_slices, pre_all).astype(BF16)
    grad_query = weight_grads[:, :width]
    grad_key = weight_grads[:, width : 2 * width]
    grad_value = weight_grads[:, 2 * width :]
    grad_output = ein("td,ti->di", grad_slices, rows_all).astype(BF16)
    return (input_grad, grad_query, grad_key, grad_value, grad_output)


def solution(mesh):
    return jax.shard_map(
        local,
        mesh=mesh,
        in_specs=(P("ctx", "head"),) * 2 + (P(None, "head"),) * 4,
        out_specs=(P("ctx", "head"),) * 5,
        check_vma=False,
    )
```

time: 563 us -> 326 us (0.58)
  waiting for transfers between devices: 395 us -> 168 us
  starting transfers between devices: 0.38 us -> 27.2 us
  other arithmetic: 25.3 us -> 6.69 us
  matrix products: 93.2 us -> 75 us
  local copies, waits for them, and re-layouts: 20.4 us -> 33.4 us
  between operations: 14 us -> 1.35 us
    reduce_scatter x2 -> x0, waiting for transfers between devices: 272 us -> none  [the longest x1 200 us: local(): lax.psum_scatter(jnp.concatenate([jnp.einsum('td,ti->di', whole_tokens, q...]
    ppermute x0 -> x33, waiting for transfers between devices: none -> 168 us  [the longest x12 72.1 us: across(): return lax.ppermute(x, 'ctx', [(i, i ^ j) for i in range(self.nc)])]
    all_gather x2 -> x0, waiting for transfers between devices: 121 us -> none  [the longest x1 77.5 us: local(): lax.all_gather(tokens, 'head', axis=1, tiled=True)]
    ppermute x0 -> x33, starting transfers between devices: none -> 27.2 us  [the longest x12 13.7 us: along_y(): lax.ppermute(x, 'head', [(i, i // Y * Y + (i + 1) % Y) for i in range(sel...]
    concatenate x1, other arithmetic: 22.8 us -> 0.05 us  [local(): pre = jnp.concatenate([query_pre, key_pre, value_pre], axis=1)]
    dot_general x23 -> x42, matrix products: 93.2 us -> 75 us  [the longest x38 50.2 us: ein(): return jnp.einsum(spec, left, right, preferred_element_type=F32)]
    dynamic_update_slice x0 -> x15, local copies, waits for them, and re-layouts: none -> 14.3 us  [gather_features(): whole = lax.dynamic_update_slice(whole, part, (0, place * cols))]
    unnamed x10 -> x50, local copies, waits for them, and re-layouts: 14.3 us -> 0.83 us
  transfers between devices with their start and end apart: 4 -> 33, of which waited for: 4 -> 17; matrix products, arithmetic and copies ran while one was open for 13% -> 21% of each run, Pallas kernels for 0% -> 0%
where the time goes in v1:
time: 326 us
  waiting for transfers between devices  168 us (52%)
  matrix products  75 us (23%)
  local copies, waits for them, and re-layouts  33.4 us (10%)
  starting transfers between devices  27.2 us (8%)
  blocking collectives  14.6 us (4%)
  other arithmetic  6.69 us (2%)
    ppermute x12, waiting for transfers between devices, across(): return lax.ppermute(x, 'ctx', [(i, i ^ j) for i in range(self.nc)])  72.1 us
    ppermute x9, waiting for transfers between devices, along_z(): lax.ppermute(x, 'head', [(i, (i + self.Y) % self.nh) for i in range(self....  61.9 us
    dot_general x38, matrix products, ein(): return jnp.einsum(spec, left, right, preferred_element_type=F32)  50.2 us
    ppermute x12, waiting for transfers between devices, along_y(): lax.ppermute(x, 'head', [(i, i // Y * Y + (i + 1) % Y) for i in range(sel...  33.5 us
    all_gather x2, blocking collectives, states(): every = lax.all_gather(x.astype(BF16), 'ctx').astype(F32)  14.6 us
    dynamic_update_slice x15, local copies, waits for them, and re-layouts, gather_features(): whole = lax.dynamic_update_slice(whole, part, (0, place * cols))  14.3 us
    ppermute x12, starting transfers between devices, along_y(): lax.ppermute(x, 'head', [(i, i // Y * Y + (i + 1) % Y) for i in range(sel...  13.7 us
    dot_general x1, matrix products, local(): jnp.dot(whole_grads, w_output, preferred_element_type=F32)  8.05 us
  transfers between devices with their start and end apart: 33, of which 17 were waited for; matrix products, arithmetic and copies ran while one was open for 21% of the time, Pallas kernels for 0%

profile of v1, /device:TPU:0, one launch (start us, length us, event | category | flops | bytes accessed | tf_op | source)
XLA Modules:
  0.0 325.8 jit_solution(17144003872773846081)
XLA Ops:
  10.8 7.9 %collective-permute-done.1 = bf16[256,1024]{1,0:T(8,128)(2,1)S(1)} collective-permute-done((bf16[256,1024]{1,0:T(8,128)(2,1)}, bf16[256,1024]{1,0:T(8,128)(2,1)S(1)}, u32[]{:S(2)}, u32[]{:S(2)}) %collective-permute-start.1) | collective-permute-done | bytes 524320 | tf_op jit(solution)/shard_map/ppermute | solution.py:43
  18.7 11.2 %collective-permute-done.8 = bf16[256,1024]{1,0:T(8,128)(2,1)S(1)} collective-permute-done((bf16[256,1024]{1,0:T(8,128)(2,1)}, bf16[256,1024]{1,0:T(8,128)(2,1)S(1)}, u32[]{:S(2)}, u32[]{:S(2)}) %collective-permute-start.8) | collective-permute-done | bytes 524320 | tf_op jit(solution)/shard_map/ppermute | solution.py:43
  37.1 4.1 %collective-permute-done.3 = bf16[256,1024]{1,0:T(8,128)(2,1)S(1)} collective-permute-done((bf16[256,1024]{1,0:T(8,128)(2,1)S(1)}, bf16[256,1024]{1,0:T(8,128)(2,1)S(1)}, u32[]{:S(2)}, u32[]{:S(2)}) %collective-permute-start.3) | collective-permute-done | bytes 524320 | tf_op jit(solution)/shard_map/ppermute | solution.py:43
  41.2 11.3 %collective-permute-done.10 = bf16[256,1024]{1,0:T(8,128)(2,1)} collective-permute-done((bf16[256,1024]{1,0:T(8,128)(2,1)S(1)}, bf16[256,1024]{1,0:T(8,128)(2,1)}, u32[]{:S(2)}, u32[]{:S(2)}) %collective-permute-start.10) | collective-permute-done | bytes 524320 | tf_op jit(solution)/shard_map/ppermute | solution.py:43
  60.0 3.6 %collective-permute-done.5 = bf16[256,1024]{1,0:T(8,128)(2,1)S(1)} collective-permute-done((bf16[256,1024]{1,0:T(8,128)(2,1)S(1)}, bf16[256,1024]{1,0:T(8,128)(2,1)S(1)}, u32[]{:S(2)}, u32[]{:S(2)}) %collective-permute-start.5) | collective-permute-done | bytes 524320 | tf_op jit(solution)/shard_map/ppermute | solution.py:43
  65.4 8.6 %collective-permute-done.12 = bf16[256,1024]{1,0:T(8,128)(2,1)S(1)} collective-permute-done((bf16[256,1024]{1,0:T(8,128)(2,1)}, bf16[256,1024]{1,0:T(8,128)(2,1)S(1)}, u32[]{:S(2)}, u32[]{:S(2)}) %collective-permute-start.12) | collective-permute-done | bytes 524320 | tf_op jit(solution)/shard_map/ppermute | solution.py:43
  78.2 3.3 %collective-permute-done.4 = bf16[256,1024]{1,0:T(8,128)(2,1)S(1)} collective-permute-done((bf16[256,1024]{1,0:T(8,128)(2,1)S(1)}, bf16[256,1024]{1,0:T(8,128)(2,1)S(1)}, u32[]{:S(2)}, u32[]{:S(2)}) %collective-permute-start.4) | collective-permute-done | bytes 524320 | tf_op jit(solution)/shard_map/ppermute | solution.py:47
  83.2 9.5 %collective-permute-done.6 = bf16[256,1024]{1,0:T(8,128)(2,1)S(1)} collective-permute-done((bf16[256,1024]{1,0:T(8,128)(2,1)S(1)}, bf16[256,1024]{1,0:T(8,128)(2,1)S(1)}, u32[]{:S(2)}, u32[]{:S(2)}) %collective-permute-start.6) | collective-permute-done | bytes 524320 | tf_op jit(solution)/shard_map/ppermute | solution.py:47
  92.7 9.1 %collective-permute-done.13 = bf16[256,1024]{1,0:T(8,128)(2,1)S(1)} collective-permute-done((bf16[256,1024]{1,0:T(8,128)(2,1)S(1)}, bf16[256,1024]{1,0:T(8,128)(2,1)S(1)}, u32[]{:S(2)}, u32[]{:S(2)}) %collective-permute-start.13) | collective-permute-done | bytes 524320 | tf_op jit(solution)/shard_map/ppermute | solution.py:47
  102.8 7.5 %fusion.36 = bf16[32,4,8,128]{3,2,1,0:T(8,128)(2,1)S(1)} fusion(bf16[256,8192]{1,0:T(8,128)(2,1)} %get-tuple-element.25, bf16[8192,512]{1,0:T(8,128)(2,1)} %param.10), kind=kOutput, calls=%fused_computation.58 | convolution fusion | flops 2147614720 | bytes 12845056 | tf_op jit(solution)/shard_map/dot_general | solution.py:102
  110.4 4.7 %fusion.124 = f32[256,512]{1,0:T(8,128)S(1)} fusion(bf16[256,8192]{1,0:T(8,128)(2,1)} %get-tuple-element.25, bf16[8192,512]{1,0:T(8,128)(2,1)S(1)} %bitcast.124), kind=kOutput, calls=%fused_computation.196 | convolution fusion | flops 2147483648 | bytes 13107200 | tf_op jit(solution)/shard_map/dot_general | solution.py:101
  115.5 7.1 %all-gather = bf16[16,128,128]{2,1,0:T(8,128)(2,1)S(1)} all-gather(bf16[4,128,128]{2,1,0:T(8,128)(2,1)S(1)} %convolution_convert_fusion.3), channel_id=2, replica_groups=mesh['ctx'=4,'head'=8] {'ctx'}, dimensions={0}, use_global_device_ids=true | all-gather | bytes 655360 | tf_op jit(solution)/shard_map/all_gather | solution.py:88
  122.6 4.6 %select_convert_fusion.1 = (bf16[256,512]{1,0:T(8,128)(2,1)S(1)}, f32[256,512]{1,0:T(8,128)S(1)}) fusion(bf16[256,8192]{1,0:T(8,128)(2,1)} %get-tuple-element.25, bf16[8192,512]{1,0:T(8,128)(2,1)S(1)} %bitcast.120), kind=kOutput, calls=%fused_computation.118 | convolution fusion | flops 2148139008 | bytes 13369344 | tf_op jit(solution)/shard_map/dot_general | solution.py:100
  128.5 8.1 %multiply_reduce_fusion = (f32[4,256]{1,0:T(4,128)S(1)}, f32[256,512]{0,1:T(8,128)S(1)}) fusion(f32[4,256,128]{1,2,0:T(8,128)S(1)} %get-tuple-element.21, f32[4,256]{1,0:T(4,128)S(1)} %get-tuple-element.17, bf16[256,8192]{1,0:T(8,128)(2,1)} %get-tuple-element.24, bf16[8192,512]{1,0:T(8,128)(2,1)} %param.11), kind=kOutput, calls=%fused_computation.114 | convolution fusion | flops 2147875840 | bytes 13639680 | tf_op jit(solution)/shard_map/dot_general | solution.py:119
  146.3 7.5 %all-gather.1 = bf16[16,128,128]{2,1,0:T(8,128)(2,1)S(1)} all-gather(bf16[4,128,128]{2,1,0:T(8,128)(2,1)S(1)} %convolution_convert_fusion.2), channel_id=3, replica_groups=mesh['ctx'=4,'head'=8] {'ctx'}, dimensions={0}, use_global_device_ids=true | all-gather | bytes 655360 | tf_op jit(solution)/shard_map/all_gather | solution.py:88
  181.1 3.6 %constant_dynamic-slice_fusion.7 = (bf16[256,2048]{1,0:T(8,128)(2,1)}, bf16[256,2048]{1,0:T(8,128)(2,1)S(1)}, bf16[256,2048]{1,0:T(8,128)(2,1)S(1)}, bf16[256,2048]{1,0:T(8,128)(2,1)S(1)}) fusion(bf16[256,8192]{1,0:T(8,128)(2,1)} %get-tuple-element.25, s32[]{:T(128)S(6)} %select_n.264, s32[]{:T(128)S(6)} %select_n.267, s32[]{:T(128)S(6)} %select_n.266, ...), kind=kLoop, calls=%fused_computation.147 | loop fusion | bytes 8388624 | tf_op jit(solution)/shard_map/dynamic_slice | solution.py:78
  192.4 4.4 %constant_dynamic-slice_fusion.3 = (bf16[256,2048]{1,0:T(8,128)(2,1)}, bf16[256,2048]{1,0:T(8,128)(2,1)}, bf16[256,2048]{1,0:T(8,128)(2,1)}, bf16[256,2048]{1,0:T(8,128)(2,1)}) fusion(bf16[256,8192]{1,0:T(8,128)(2,1)} %get-tuple-element.24, s32[]{:T(128)S(6)} %select_n.264, s32[]{:T(128)S(6)} %select_n.267, s32[]{:T(128)S(6)} %select_n.266, s32[]{:T(128)S(6)} %select_n.265), kind=kLoop, calls=%fused_computation.143 | loop fusion | bytes 8388624 | tf_op jit(solution)/shard_map/dynamic_slice | solution.py:78
  198.1 51.3 %collective-permute-done.25 = bf16[256,1536]{1,0:T(8,128)(2,1)S(1)} collective-permute-done((bf16[256,1536]{1,0:T(8,128)(2,1)S(1)}, bf16[256,1536]{1,0:T(8,128)(2,1)S(1)}, u32[]{:S(2)}, u32[]{:S(2)}) %collective-permute-start.25) | collective-permute-done | bytes 786464 | tf_op jit(solution)/shard_map/ppermute | solution.py:50
  253.7 9.6 %convolution_convert_fusion = bf16[2048,1536]{1,0:T(8,128)(2,1)S(1)} fusion(bf16[256,2048]{1,0:T(8,128)(2,1)} %copy-done.9, bf16[256,2048]{1,0:T(8,128)(2,1)} %copy-done.10, bf16[256,2048]{1,0:T(8,128)(2,1)} %copy-done.11, bf16[256,2048]{1,0:T(8,128)(2,1)} %get-tuple-element.12, bf16[256,1536]{1,0:T(8,128)(2,1)} %copy-done.12, ...), kind=kOutput, calls=%fused_computation | convolution fusion | flops 6481248256 | bytes 13631488 | tf_op jit(solution)/shard_map/td,ti->di/dot_general | solution.py:28
  266.1 3.2 collective-permute-done.18
  277.0 9.8 %collective-permute-done.19 = bf16[256,1024]{1,0:T(8,128)(2,1)S(1)} collective-permute-done((bf16[256,1024]{1,0:T(8,128)(2,1)S(1)}, bf16[256,1024]{1,0:T(8,128)(2,1)S(1)}, u32[]{:S(2)}, u32[]{:S(2)}) %collective-permute-start.19) | collective-permute-done | bytes 524320 | tf_op jit(solution)/shard_map/ppermute | solution.py:43
  288.1 20.7 %collective-permute-done.31 = bf16[256,512]{0,1:T(8,128)(2,1)S(1)} collective-permute-done((bf16[256,512]{0,1:T(8,128)(2,1)}, bf16[256,512]{0,1:T(8,128)(2,1)S(1)}, u32[]{:S(2)}, u32[]{:S(2)}) %collective-permute-start.31) | collective-permute-done | bytes 262176 | tf_op jit(solution)/shard_map/ppermute | solution.py:50
  310.5 5.0 %fusion.26 = bf16[2048,512]{1,0:T(8,128)(2,1)} fusion(bf16[256,2048]{1,0:T(8,128)(2,1)} %collective-permute-done.29, bf16[256,2048]{1,0:T(8,128)(2,1)S(1)} %collective-permute-done.28, bf16[256,2048]{1,0:T(8,128)(2,1)S(1)} %collective-permute-done.27, bf16[256,2048]{1,0:T(8,128)(2,1)S(1)} %copy-done.2, bf16[256,512]{0,1:T(8,128)(2,1)S(1)} %collective-permute-done.32, ...), kind=kOutput, calls=%fused_computation.27 | convolution fusion | flops 2169503744 | bytes 7340032 | tf_op jit(solution)/shard_map/td,ti->di/dot_general | solution.py:28
  315.5 7.1 %collective-permute-done.14 = bf16[256,1024]{1,0:T(8,128)(2,1)S(1)} collective-permute-done((bf16[256,1024]{1,0:T(8,128)(2,1)S(1)}, bf16[256,1024]{1,0:T(8,128)(2,1)S(1)}, u32[]{:S(2)}, u32[]{:S(2)}) %collective-permute-start.14) | collective-permute-done | bytes 524320 | tf_op jit(solution)/shard_map/ppermute | solution.py:47
  (181 shorter events, 101.6 us)
Async XLA Ops:
  3.7 26.2 %collective-permute-start.8 = (bf16[256,1024]{1,0:T(8,128)(2,1)}, bf16[256,1024]{1,0:T(8,128)(2,1)S(1)}, u32[]{:S(2)}, u32[]{:S(2)}) collective-permute-start(bf16[256,1024]{1,0:T(8,128)(2,1)} %param.7), channel_id=1, source_target_pairs={{0,2},{1,3},{2,4},{3,5},{4,6},{5,7},{6,0},{7,1},{8,10},{9,11},{10,... | collective-permute-start | bytes 1572872 | tf_op jit(solution)/shard_map/ppermute | solution.py:43
  5.3 47.3 %collective-permute-start = (bf16[256,1024]{1,0:T(8,128)(2,1)}, bf16[256,1024]{1,0:T(8,128)(2,1)S(1)}, u32[]{:S(2)}, u32[]{:S(2)}) collective-permute-start(bf16[256,1024]{1,0:T(8,128)(2,1)} %param.6), channel_id=1, source_target_pairs={{0,1},{1,0},{2,3},{3,2},{4,5},{5,4},{6,7},{7,6},{8,9},{9,8},{10,11... | collective-permute-start | bytes 1572872 | tf_op jit(solution)/shard_map/ppermute | solution.py:47
  6.8 28.2 %collective-permute-start.7 = (bf16[256,1024]{1,0:T(8,128)(2,1)}, bf16[256,1024]{1,0:T(8,128)(2,1)S(1)}, u32[]{:S(2)}, u32[]{:S(2)}) collective-permute-start(bf16[256,1024]{1,0:T(8,128)(2,1)} %param.7), channel_id=1, source_target_pairs={{0,1},{1,0},{2,3},{3,2},{4,5},{5,4},{6,7},{7,6},{8,9},{9,8},{10,11... | collective-permute-start | bytes 1572872 | tf_op jit(solution)/shard_map/ppermute | solution.py:47
  29.9 22.6 %collective-permute-start.10 = (bf16[256,1024]{1,0:T(8,128)(2,1)S(1)}, bf16[256,1024]{1,0:T(8,128)(2,1)}, u32[]{:S(2)}, u32[]{:S(2)}) collective-permute-start(bf16[256,1024]{1,0:T(8,128)(2,1)S(1)} %collective-permute-done.8), channel_id=1, source_target_pairs={{0,2},{1,3},{2,4},{3,5},{4,6},{5,7},{6,0},{7,1},{8,10},{9,11},{10,... | collective-permute-start | bytes 1572872 | tf_op jit(solution)/shard_map/ppermute | solution.py:43
  33.3 22.7 %collective-permute-start.9 = (bf16[256,1024]{1,0:T(8,128)(2,1)S(1)}, bf16[256,1024]{1,0:T(8,128)(2,1)S(1)}, u32[]{:S(2)}, u32[]{:S(2)}) collective-permute-start(bf16[256,1024]{1,0:T(8,128)(2,1)S(1)} %collective-permute-done.8), channel_id=1, source_target_pairs={{0,1},{1,0},{2,3},{3,2},{4,5},{5,4},{6,7},{7,6},{8,9},{9,8},{10,11... | collective-permute-start | bytes 1572872 | tf_op jit(solution)/shard_map/ppermute | solution.py:47
  35.0 24.1 %collective-permute-start.2 = (bf16[256,1024]{1,0:T(8,128)(2,1)S(1)}, bf16[256,1024]{1,0:T(8,128)(2,1)S(1)}, u32[]{:S(2)}, u32[]{:S(2)}) collective-permute-start(bf16[256,1024]{1,0:T(8,128)(2,1)S(1)} %collective-permute-done.1), channel_id=1, source_target_pairs={{0,1},{1,0},{2,3},{3,2},{4,5},{5,4},{6,7},{7,6},{8,9},{9,8},{10,11... | collective-permute-start | bytes 1572872 | tf_op jit(solution)/shard_map/ppermute | solution.py:47
  41.2 22.5 %collective-permute-start.5 = (bf16[256,1024]{1,0:T(8,128)(2,1)S(1)}, bf16[256,1024]{1,0:T(8,128)(2,1)S(1)}, u32[]{:S(2)}, u32[]{:S(2)}) collective-permute-start(bf16[256,1024]{1,0:T(8,128)(2,1)S(1)} %collective-permute-done.3), channel_id=1, source_target_pairs={{0,2},{1,3},{2,4},{3,5},{4,6},{5,7},{6,0},{7,1},{8,10},{9,11},{10,... | collective-permute-start | bytes 1572872 | tf_op jit(solution)/shard_map/ppermute | solution.py:43
  53.4 23.1 %collective-permute-start.11 = (bf16[256,1024]{1,0:T(8,128)(2,1)}, bf16[256,1024]{1,0:T(8,128)(2,1)S(1)}, u32[]{:S(2)}, u32[]{:S(2)}) collective-permute-start(bf16[256,1024]{1,0:T(8,128)(2,1)} %collective-permute-done.10), channel_id=1, source_target_pairs={{0,1},{1,0},{2,3},{3,2},{4,5},{5,4},{6,7},{7,6},{8,9},{9,8},{10,11... | collective-permute-start | bytes 1572872 | tf_op jit(solution)/shard_map/ppermute | solution.py:47
  56.1 25.4 %collective-permute-start.4 = (bf16[256,1024]{1,0:T(8,128)(2,1)S(1)}, bf16[256,1024]{1,0:T(8,128)(2,1)S(1)}, u32[]{:S(2)}, u32[]{:S(2)}) collective-permute-start(bf16[256,1024]{1,0:T(8,128)(2,1)S(1)} %collective-permute-done.3), channel_id=1, source_target_pairs={{0,1},{1,0},{2,3},{3,2},{4,5},{5,4},{6,7},{7,6},{8,9},{9,8},{10,11... | collective-permute-start | bytes 1572872 | tf_op jit(solution)/shard_map/ppermute | solution.py:47
  63.6 29.0 %collective-permute-start.6 = (bf16[256,1024]{1,0:T(8,128)(2,1)S(1)}, bf16[256,1024]{1,0:T(8,128)(2,1)S(1)}, u32[]{:S(2)}, u32[]{:S(2)}) collective-permute-start(bf16[256,1024]{1,0:T(8,128)(2,1)S(1)} %collective-permute-done.5), channel_id=1, source_target_pairs={{0,1},{1,0},{2,3},{3,2},{4,5},{5,4},{6,7},{7,6},{8,9},{9,8},{10,11... | collective-permute-start | bytes 1572872 | tf_op jit(solution)/shard_map/ppermute | solution.py:47
  74.1 27.7 %collective-permute-start.13 = (bf16[256,1024]{1,0:T(8,128)(2,1)S(1)}, bf16[256,1024]{1,0:T(8,128)(2,1)S(1)}, u32[]{:S(2)}, u32[]{:S(2)}) collective-permute-start(bf16[256,1024]{1,0:T(8,128)(2,1)S(1)} %collective-permute-done.12), channel_id=1, source_target_pairs={{0,1},{1,0},{2,3},{3,2},{4,5},{5,4},{6,7},{7,6},{8,9},{9,8},{10,11... | collective-permute-start | bytes 1572872 | tf_op jit(solution)/shard_map/ppermute | solution.py:47
  160.2 31.4 %collective-permute-start.26 = (bf16[256,1536]{1,0:T(8,128)(2,1)S(1)}, bf16[256,1536]{1,0:T(8,128)(2,1)S(1)}, u32[]{:S(2)}, u32[]{:S(2)}) collective-permute-start(bf16[256,1536]{1,0:T(8,128)(2,1)S(1)} %pad_maximum_fusion), channel_id=1, source_target_pairs={{0,24},{8,16},{16,8},{24,0},{1,25},{9,17},{17,9},{25,1},{2,26},{10... | collective-permute-start | bytes 2359304 | tf_op jit(solution)/shard_map/ppermute | solution.py:50
  165.0 25.5 %collective-permute-start.17 = (bf16[256,1024]{1,0:T(8,128)(2,1)S(1)}, bf16[256,1024]{1,0:T(8,128)(2,1)S(1)}, u32[]{:S(2)}, u32[]{:S(2)}) collective-permute-start(bf16[256,1024]{1,0:T(8,128)(2,1)S(1)} %fusion.32), channel_id=1, source_target_pairs={{0,1},{1,0},{2,3},{3,2},{4,5},{5,4},{6,7},{7,6},{8,9},{9,8},{10,11... | collective-permute-start | bytes 1572872 | tf_op jit(solution)/shard_map/ppermute | solution.py:47
  184.7 66.4 %collective-permute-start.23 = (bf16[256,2048]{1,0:T(8,128)(2,1)S(1)}, bf16[256,2048]{1,0:T(8,128)(2,1)S(1)}, u32[]{:S(2)}, u32[]{:S(2)}) collective-permute-start(bf16[256,2048]{1,0:T(8,128)(2,1)S(1)} %get-tuple-element.13), channel_id=1, source_target_pairs={{0,24},{8,16},{16,8},{24,0},{1,25},{9,17},{17,9},{25,1},{2,26},{10... | collective-permute-start | bytes 3145736 | tf_op jit(solution)/shard_map/ppermute | solution.py:50
  185.4 67.0 %collective-permute-start.22 = (bf16[256,2048]{1,0:T(8,128)(2,1)S(1)}, bf16[256,2048]{1,0:T(8,128)(2,1)S(1)}, u32[]{:S(2)}, u32[]{:S(2)}) collective-permute-start(bf16[256,2048]{1,0:T(8,128)(2,1)S(1)} %get-tuple-element.14), channel_id=1, source_target_pairs={{0,16},{8,24},{16,0},{24,8},{1,17},{9,25},{17,1},{25,9},{2,18},{10... | collective-permute-start | bytes 3145736 | tf_op jit(solution)/shard_map/ppermute | solution.py:50
  186.2 66.5 %collective-permute-start.21 = (bf16[256,2048]{1,0:T(8,128)(2,1)S(1)}, bf16[256,2048]{1,0:T(8,128)(2,1)S(1)}, u32[]{:S(2)}, u32[]{:S(2)}) collective-permute-start(bf16[256,2048]{1,0:T(8,128)(2,1)S(1)} %get-tuple-element.15), channel_id=1, source_target_pairs={{0,8},{8,0},{16,24},{24,16},{1,9},{9,1},{17,25},{25,17},{2,10},{10... | collective-permute-start | bytes 3145736 | tf_op jit(solution)/shard_map/ppermute | solution.py:50
  190.4 59.0 %collective-permute-start.25 = (bf16[256,1536]{1,0:T(8,128)(2,1)S(1)}, bf16[256,1536]{1,0:T(8,128)(2,1)S(1)}, u32[]{:S(2)}, u32[]{:S(2)}) collective-permute-start(bf16[256,1536]{1,0:T(8,128)(2,1)S(1)} %pad_maximum_fusion), channel_id=1, source_target_pairs={{0,16},{8,24},{16,0},{24,8},{1,17},{9,25},{17,1},{25,9},{2,18},{10... | collective-permute-start | bytes 2359304 | tf_op jit(solution)/shard_map/ppermute | solution.py:50
  191.6 58.7 %collective-permute-start.24 = (bf16[256,1536]{1,0:T(8,128)(2,1)S(1)}, bf16[256,1536]{1,0:T(8,128)(2,1)S(1)}, u32[]{:S(2)}, u32[]{:S(2)}) collective-permute-start(bf16[256,1536]{1,0:T(8,128)(2,1)S(1)} %pad_maximum_fusion), channel_id=1, source_target_pairs={{0,8},{8,0},{16,24},{24,16},{1,9},{9,1},{17,25},{25,17},{2,10},{10... | collective-permute-start | bytes 2359304 | tf_op jit(solution)/shard_map/ppermute | solution.py:50
  251.1 25.1 %collective-permute-start.15 = (bf16[256,1024]{1,0:T(8,128)(2,1)}, bf16[256,1024]{1,0:T(8,128)(2,1)}, u32[]{:S(2)}, u32[]{:S(2)}) collective-permute-start(bf16[256,1024]{1,0:T(8,128)(2,1)} %fusion.30), channel_id=1, source_target_pairs={{0,1},{1,0},{2,3},{3,2},{4,5},{5,4},{6,7},{7,6},{8,9},{9,8},{10,11... | collective-permute-start | bytes 1572872 | tf_op jit(solution)/shard_map/ppermute | solution.py:47
  252.4 58.1 %collective-permute-start.29 = (bf16[256,2048]{1,0:T(8,128)(2,1)}, bf16[256,2048]{1,0:T(8,128)(2,1)}, u32[]{:S(2)}, u32[]{:S(2)}) collective-permute-start(bf16[256,2048]{1,0:T(8,128)(2,1)} %get-tuple-element.9), channel_id=1, source_target_pairs={{0,24},{8,16},{16,8},{24,0},{1,25},{9,17},{17,9},{25,1},{2,26},{10... | collective-permute-start | bytes 3145736 | tf_op jit(solution)/shard_map/ppermute | solution.py:50
  265.3 45.2 %collective-permute-start.28 = (bf16[256,2048]{1,0:T(8,128)(2,1)}, bf16[256,2048]{1,0:T(8,128)(2,1)S(1)}, u32[]{:S(2)}, u32[]{:S(2)}) collective-permute-start(bf16[256,2048]{1,0:T(8,128)(2,1)} %get-tuple-element.10), channel_id=1, source_target_pairs={{0,16},{8,24},{16,0},{24,8},{1,17},{9,25},{17,1},{25,9},{2,18},{10... | collective-permute-start | bytes 3145736 | tf_op jit(solution)/shard_map/ppermute | solution.py:50
  269.3 41.1 %collective-permute-start.27 = (bf16[256,2048]{1,0:T(8,128)(2,1)}, bf16[256,2048]{1,0:T(8,128)(2,1)S(1)}, u32[]{:S(2)}, u32[]{:S(2)}) collective-permute-start(bf16[256,2048]{1,0:T(8,128)(2,1)} %get-tuple-element.11), channel_id=1, source_target_pairs={{0,8},{8,0},{16,24},{24,16},{1,9},{9,1},{17,25},{25,17},{2,10},{10... | collective-permute-start | bytes 3145736 | tf_op jit(solution)/shard_map/ppermute | solution.py:50
  276.2 32.7 %collective-permute-start.31 = (bf16[256,512]{0,1:T(8,128)(2,1)}, bf16[256,512]{0,1:T(8,128)(2,1)S(1)}, u32[]{:S(2)}, u32[]{:S(2)}) collective-permute-start(bf16[256,512]{0,1:T(8,128)(2,1)} %bitcast.25), channel_id=1, source_target_pairs={{0,16},{8,24},{16,0},{24,8},{1,17},{9,25},{17,1},{25,9},{2,18},{10... | collective-permute-start | bytes 786440 | tf_op jit(solution)/shard_map/ppermute | solution.py:50
  286.8 22.7 %collective-permute-start.30 = (bf16[256,512]{0,1:T(8,128)(2,1)}, bf16[256,512]{0,1:T(8,128)(2,1)S(1)}, u32[]{:S(2)}, u32[]{:S(2)}) collective-permute-start(bf16[256,512]{0,1:T(8,128)(2,1)} %bitcast.25), channel_id=1, source_target_pairs={{0,8},{8,0},{16,24},{24,16},{1,9},{9,1},{17,25},{25,17},{2,10},{10... | collective-permute-start | bytes 786440 | tf_op jit(solution)/shard_map/ppermute | solution.py:50
  (34 other events, 570.9 us)

commit v2 on v1

v2 whole, which is shorter than its diff:
```python
import functools

import jax
import jax.numpy as jnp
from jax import lax
from jax.experimental import pallas as pl
from jax.experimental.pallas import tpu as pltpu
from jax.sharding import PartitionSpec as P

HD = 128
F32 = jnp.float32
BF16 = jnp.bfloat16


def tie(x, *others):
    return lax.optimization_barrier((x,) + others)[0]


class Lines:
    def __init__(self):
        self.nh = lax.axis_size("head")
        self.nc = lax.axis_size("ctx")
        self.Z = 4 if self.nh % 4 == 0 else 1
        self.Y = self.nh // self.Z
        here = lax.axis_index("head")
        self.c = lax.axis_index("ctx")
        self.z = here // self.Y
        self.y = here % self.Y

    def along_z(self, x):
        return lax.ppermute(x, "head", [(i, (i + self.Y) % self.nh) for i in range(self.nh)])

    def along_y(self, x):
        Y = self.Y
        return lax.ppermute(x, "head", [(i, i // Y * Y + (i + 1) % Y) for i in range(self.nh)])

    def across(self, x, j):
        return lax.ppermute(x, "ctx", [(i, i ^ j) for i in range(self.nc)])

    def shard(self, k, j):
        return ((self.z - k) % self.Z) * self.Y + (self.y - j) % self.Y


def gather_piece(at, x, z_first, after=()):
    parts = []
    if z_first:
        now = x
        for k in range(at.Z):
            if k:
                now = at.along_z(tie(now, *after) if after and k == 1 else now)
            side = now
            for j in range(at.Y):
                if j:
                    side = at.along_y(side)
                parts.append((k, at.shard(k, j), side))
        return parts
    sides = [x]
    for _ in range(at.Y - 1):
        sides.append(at.along_y(sides[-1]))
    now = jnp.concatenate(sides, axis=1)
    cols = x.shape[1]
    for k in range(at.Z):
        if k:
            now = at.along_z(tie(now, *after) if after and k == 1 else now)
        for j in range(at.Y):
            parts.append((k, at.shard(k, j), now[:, j * cols : (j + 1) * cols]))
    return parts


def place(whole, parts, row, cols):
    for _, where, part in parts:
        whole = lax.dynamic_update_slice(whole, part, (row, where * cols))
    return whole


def slices_out(at, whole):
    width = whole.shape[1] // at.nc
    out = []
    for j in range(at.nc):
        piece = lax.dynamic_slice_in_dim(whole, (at.c ^ j) * width, width, 1)
        out.append(at.across(piece, j) if j else piece)
    return out


def blocks_out(at, x):
    return [at.across(x, j) if j else x for j in range(at.nc)]


def mm(a, b, ca, cb):
    return lax.dot_general(a, b, (((ca,), (cb,)), ((), ())), preferred_element_type=F32)


def slope(values):
    return jnp.where(values > 0, 1.0, jnp.exp(jnp.minimum(values, 0.0)))


def feature(values):
    return jnp.where(values > 0, values + 1.0, jnp.exp(jnp.minimum(values, 0.0)))


def causal(values):
    rows = lax.broadcasted_iota(jnp.int32, values.shape, 0)
    cols = lax.broadcasted_iota(jnp.int32, values.shape, 1)
    return jnp.where(rows >= cols, values, 0.0)


def per_head(kernel, number, ins, outs, scalars=(), flops=0):
    def spec(shape, kind):
        if kind == "c":
            return pl.BlockSpec((shape[0], HD), lambda h, *_: (0, h))
        if kind == "r":
            return pl.BlockSpec((shape[0] // number, shape[1]), lambda h, *_: (h, 0))
        return pl.BlockSpec((shape[0], shape[1], HD), lambda h, *_: (0, 0, h))

    arrays = [a for a, _ in ins]
    moved = sum(a.size * a.dtype.itemsize for a in arrays)
    shapes = [jax.ShapeDtypeStruct(s, d) for s, d, _ in outs]
    moved += sum(s.size * s.dtype.itemsize for s in shapes)
    return pl.pallas_call(
        kernel,
        out_shape=shapes,
        grid_spec=pltpu.PrefetchScalarGridSpec(
            num_scalar_prefetch=len(scalars),
            grid=(number,),
            in_specs=[spec(a.shape, k) for a, k in ins],
            out_specs=[spec(s, k) for s, _, k in outs],
        ),
        cost_estimate=pl.CostEstimate(flops=flops, bytes_accessed=moved, transcendentals=0),
    )(*scalars, *arrays)


def forward_kernel(q_ref, k_ref, v_ref, qf_ref, kf_ref, vf_ref, sc_ref, in_ref, kv_ref):
    qf = feature(q_ref[...]).astype(BF16)
    kf = feature(k_ref[...]).astype(BF16)
    vf = v_ref[...].astype(BF16)
    scores = causal(mm(qf, kf, 1, 1)).astype(BF16)
    qf_ref[...] = qf
    kf_ref[...] = kf
    vf_ref[...] = vf
    sc_ref[...] = scores
    in_ref[...] = mm(scores, vf, 1, 0)
    kv_ref[...] = mm(kf, vf, 0, 0).astype(BF16)


def state_sum(c, refs, later):
    total = jnp.zeros(refs[0].shape, F32)
    for j, ref in enumerate(refs):
        other = c ^ (j + 1)
        use = (other > c) if later else (other < c)
        total = total + jnp.where(use, ref[...].astype(F32), 0.0)
    return total.astype(BF16)


def norm_kernel(nc, c_ref, in_ref, qf_ref, *refs):
    kv, (no_ref, sl_ref, ar_ref, pf_ref) = refs[: nc - 1], refs[nc - 1 :]
    prefix = state_sum(c_ref[0], kv, False)
    attended = in_ref[...] + mm(qf_ref[...], prefix, 1, 0)
    scale = lax.rsqrt(jnp.mean(attended * attended, axis=1, keepdims=True) + 1e-06)
    normed = attended * scale
    no_ref[...] = normed
    sl_ref[...] = jnp.broadcast_to(scale, normed.shape)
    ar_ref[...] = normed.astype(BF16)
    pf_ref[...] = prefix


def delta_kernel(ga_ref, gb_ref, no_ref, sl_ref, qf_ref, od_ref, qg_ref):
    grad = ga_ref[...] + gb_ref[...]
    normed = no_ref[...]
    mean = jnp.mean(grad * normed, axis=1, keepdims=True)
    delta = (sl_ref[...] * (grad - normed * mean)).astype(BF16)
    od_ref[...] = delta
    qg_ref[...] = mm(qf_ref[...], delta, 0, 0).astype(BF16)


def inner_kernel(
    od_ref, qf_ref, kf_ref, vf_ref, sc_ref, pf_ref, q_ref, qp_ref, fk_ref, fv_ref
):
    delta = od_ref[...]
    score_grad = causal(mm(delta, vf_ref[...], 1, 1)).astype(BF16)
    feat_q = mm(score_grad, kf_ref[...], 1, 0) + mm(delta, pf_ref[...], 1, 1)
    qp_ref[...] = (feat_q * slope(q_ref[...])).astype(BF16)
    fk_ref[...] = mm(score_grad, qf_ref[...], 0, 0)
    fv_ref[...] = mm(sc_ref[...], delta, 0, 0)


def outer_kernel(nc, c_ref, fk_ref, fv_ref, kf_ref, vf_ref, k_ref, *refs):
    qg, (kv_ref,) = refs[: nc - 1], refs[nc - 1 :]
    suffix = state_sum(c_ref[0], qg, True)
    feat_k = fk_ref[...] + mm(vf_ref[...], suffix, 1, 1)
    feat_v = fv_ref[...] + mm(kf_ref[...], suffix, 1, 0)
    kv_ref[0] = (feat_k * slope(k_ref[...])).astype(BF16)
    kv_ref[1] = feat_v.astype(BF16)


def part_kernel(s_ref, q_ref, kv_ref, wq_ref, wk_ref, wv_ref, a_ref, b_ref):
    total = mm(q_ref[...], wq_ref[...], 1, 1)
    total = total + mm(kv_ref[0], wk_ref[...], 1, 1)
    total = total + mm(kv_ref[1], wv_ref[...], 1, 1)
    half = a_ref.shape[0]
    a_ref[...] = total[:half].astype(a_ref.dtype)
    b_ref[...] = total[half:].astype(b_ref.dtype)


def part_of(where, query_pre, kv_pre, weights, cols, dtype):
    rows, width = query_pre.shape
    tile = min(512, cols)
    count = cols // tile
    weight = pl.BlockSpec((tile, width), lambda i, s: (s[0] * count + i, 0))
    out = pl.BlockSpec((rows // 2, tile), lambda i, s: (0, i))
    return pl.pallas_call(
        part_kernel,
        out_shape=[jax.ShapeDtypeStruct((rows // 2, cols), dtype)] * 2,
        grid_spec=pltpu.PrefetchScalarGridSpec(
            num_scalar_prefetch=1,
            grid=(count,),
            in_specs=[
                pl.BlockSpec((rows, width), lambda i, s: (0, 0)),
                pl.BlockSpec((2, rows, width), lambda i, s: (0, 0, 0)),
                weight,
                weight,
                weight,
            ],
            out_specs=[out, out],
        ),
        cost_estimate=pl.CostEstimate(
            flops=6 * rows * width * cols, bytes_accessed=6 * cols * width, transcendentals=0
        ),
    )(jnp.reshape(where, (1,)).astype(jnp.int32), query_pre, kv_pre, *weights)


def local(tokens, out_grad, w_query, w_key, w_value, w_output):
    at = Lines()
    length, cols = tokens.shape
    width = w_query.shape[1]
    number = width // HD
    half = length // 2
    own = jnp.reshape(at.c, (1,)).astype(jnp.int32)

    token_a = gather_piece(at, tokens[:half], True)
    token_b = gather_piece(at, tokens[half:], True)
    last = [p for k, _, p in token_a if k == at.Z - 1][:1]
    cut = length * 5 // 8
    grad_a = gather_piece(at, out_grad[:cut], True, last)
    grad_b = gather_piece(at, out_grad[cut:], False, last)

    blank = jnp.zeros((length, cols * at.nh), BF16)
    whole_tokens = place(place(blank, token_a, 0, cols), token_b, half, cols)
    token_slices = slices_out(at, whole_tokens)
    query_lin = jnp.dot(whole_tokens, w_query, preferred_element_type=F32)
    key_lin = jnp.dot(whole_tokens, w_key, preferred_element_type=F32)
    value_lin = jnp.dot(whole_tokens, w_value, preferred_element_type=F32)

    columns = (length, width)
    square = (number * HD, HD)
    query_feat, key_feat, value_feat, scores, intra, local_kv = per_head(
        forward_kernel,
        number,
        [(query_lin, "c"), (key_lin, "c"), (value_lin, "c")],
        [(columns, BF16, "c")] * 3
        + [((number * length, length), BF16, "r"), (columns, F32, "c"), (square, BF16, "r")],
        flops=4 * length * length * width,
    )
    before = [at.across(local_kv, j) for j in range(1, at.nc)]
    normed, scale, attn_rows, prefix = per_head(
        functools.partial(norm_kernel, at.nc),
        number,
        [(intra, "c"), (query_feat, "c")] + [(b, "r") for b in before],
        [(columns, F32, "c"), (columns, F32, "c"), (columns, BF16, "c"), (square, BF16, "r")],
        (own,),
        flops=2 * length * HD * width,
    )
    rows_all = blocks_out(at, attn_rows)

    early = [[p for p in g if p[0] < at.Z - 1] for g in (grad_a, grad_b)]
    late = [[p for p in g if p[0] == at.Z - 1] for g in (grad_a, grad_b)]
    most_grads = place(place(blank, early[0], 0, cols), early[1], cut, cols)
    most_grads = tie(most_grads, attn_rows)
    grad_most = jnp.dot(most_grads, w_output, preferred_element_type=F32)
    whole_grads = place(place(most_grads, late[0], 0, cols), late[1], cut, cols)
    group = at.Y * cols
    start = ((at.z + 1) % at.Z) * group
    grad_last = jnp.dot(
        lax.dynamic_slice_in_dim(whole_grads, start, group, 1),
        lax.dynamic_slice_in_dim(w_output, start, group, 0),
        preferred_element_type=F32,
    )
    grad_slices = slices_out(at, whole_grads)
    out_delta, local_qg = per_head(
        delta_kernel,
        number,
        [(grad_most, "c"), (grad_last, "c"), (normed, "c"), (scale, "c"), (query_feat, "c")],
        [(columns, BF16, "c"), (square, BF16, "r")],
        flops=2 * length * HD * width,
    )
    after = [at.across(local_qg, j) for j in range(1, at.nc)]
    query_pre, inner_k, inner_v = per_head(
        inner_kernel,
        number,
        [(out_delta, "c"), (query_feat, "c"), (key_feat, "c"), (value_feat, "c")]
        + [(scores, "r"), (prefix, "r"), (query_lin, "c")],
        [(columns, BF16, "c"), (columns, F32, "c"), (columns, F32, "c")],
        flops=8 * length * length * width,
    )
    query_all = blocks_out(at, query_pre)
    (kv_pre,) = per_head(
        functools.partial(outer_kernel, at.nc),
        number,
        [(inner_k, "c"), (inner_v, "c"), (key_feat, "c"), (value_feat, "c"), (key_lin, "c")]
        + [(a, "r") for a in after],
        [((2, length, width), BF16, "h")],
        (own,),
        flops=4 * length * HD * width,
    )
    kv_pre, *token_slices = lax.optimization_barrier((kv_pre, *token_slices))
    kv_all = blocks_out(at, kv_pre)

    weights = (w_query, w_key, w_value)
    total = None
    for k in range(1, at.Z + 1):
        held = None
        for j in range(1, at.Y + 1):
            dtype = BF16 if j == 1 and j < at.Y else F32
            mine = part_of(at.shard(k, j), query_pre, kv_pre, weights, cols, dtype)
            if held is not None:
                mine = [m + h.astype(F32) for m, h in zip(mine, held)]
            held = mine
            if j < at.Y:
                held = [at.along_y(h.astype(BF16)) for h in held]
        if total is not None:
            held = [h + t.astype(F32) for h, t in zip(held, total)]
        total = [h.astype(BF16) for h in held]
        if k < at.Z:
            total = [at.along_z(t) for t in total]
    input_grad = jnp.concatenate(total, axis=0)

    def contract(left, right):
        return jnp.einsum("td,ti->di", left, right, preferred_element_type=F32).astype(BF16)

    tokens_cat = jnp.concatenate(token_slices, axis=0)
    grad_query = contract(tokens_cat, jnp.concatenate(query_all, axis=0))
    kv_cat = jnp.concatenate(kv_all, axis=1)
    grad_key = contract(tokens_cat, kv_cat[0])
    grad_value = contract(tokens_cat, kv_cat[1])
    grad_output = contract(
        jnp.concatenate(grad_slices, axis=0), jnp.concatenate(rows_all, axis=0)
    )
    return (input_grad, grad_query, grad_key, grad_value, grad_output)


def solution(mesh):
    return jax.shard_map(
        local,
        mesh=mesh,
        in_specs=(P("ctx", "head"),) * 2 + (P(None, "head"),) * 4,
        out_specs=(P("ctx", "head"),) * 5,
        check_vma=False,
    )
```

time: 326 us -> 323 us (level)
  Pallas kernels: 0 us -> 50.7 us
  waiting for transfers between devices: 168 us -> 121 us
  matrix products: 75 us -> 48.6 us
  starting transfers between devices: 27.2 us -> 51.8 us
  blocking collectives: 14.6 us -> 0 us
  local copies, waits for them, and re-layouts: 33.4 us -> 47.1 us
  other arithmetic: 6.69 us -> 1.53 us
    pallas_call x0 -> x13, Pallas kernels: none -> 50.7 us  [the longest x8 30.1 us: part_of(): pl.pallas_call(part_kernel, out_shape=[jax.ShapeDtypeStruct((rows // 2, c...]
    ppermute x12 -> x21, waiting for transfers between devices: 72.1 us -> 38.4 us  [across(): return lax.ppermute(x, 'ctx', [(i, i ^ j) for i in range(self.nc)])]
    dot_general x39 -> x6, matrix products: 58.3 us -> 29.8 us  [the longest x4 18.6 us: contract(): jnp.einsum('td,ti->di', left, right, preferred_element_type=F32)]
    all_gather x2 -> x0, blocking collectives: 14.6 us -> none  [states(): every = lax.all_gather(x.astype(BF16), 'ctx').astype(F32)]
    ppermute x9 -> x18, waiting for transfers between devices: 61.9 us -> 49 us  [along_z(): lax.ppermute(x, 'head', [(i, (i + self.Y) % self.nh) for i in range(self....]
    ppermute x12 -> x21, starting transfers between devices: 13.7 us -> 25 us  [along_y(): lax.ppermute(x, 'head', [(i, i // Y * Y + (i + 1) % Y) for i in range(sel...]
    ppermute x12 -> x21, starting transfers between devices: 6.77 us -> 15.7 us  [across(): return lax.ppermute(x, 'ctx', [(i, i ^ j) for i in range(self.nc)])]
    dynamic_update_slice x15 -> x29, local copies, waits for them, and re-layouts: 14.3 us -> 21.6 us  [place(): whole = lax.dynamic_update_slice(whole, part, (row, where * cols))]
  transfers between devices with their start and end apart: 33 -> 60, of which waited for: 17 -> 27; matrix products, arithmetic and copies ran while one was open for 21% -> 28% of each run, Pallas kernels for 0% -> 16%
where the time goes in v2:
time: 323 us; the launch traced here: 322 us
  waiting for transfers between devices  121 us (37%)
  starting transfers between devices  51.8 us (16%)
  Pallas kernels  50.7 us (16%)
  matrix products  48.6 us (15%)
  local copies, waits for them, and re-layouts  47.1 us (15%)
    ppermute x18, waiting for transfers between devices, along_z(): lax.ppermute(x, 'head', [(i, (i + self.Y) % self.nh) for i in range(self....  49 us
    ppermute x21, waiting for transfers between devices, across(): return lax.ppermute(x, 'ctx', [(i, i ^ j) for i in range(self.nc)])  38.4 us
    ppermute x21, waiting for transfers between devices, along_y(): lax.ppermute(x, 'head', [(i, i // Y * Y + (i + 1) % Y) for i in range(sel...  34 us
    pallas_call x8, Pallas kernels, part_of(): pl.pallas_call(part_kernel, out_shape=[jax.ShapeDtypeStruct((rows // 2, c...  30.1 us
    ppermute x21, starting transfers between devices, along_y(): lax.ppermute(x, 'head', [(i, i // Y * Y + (i + 1) % Y) for i in range(sel...  25 us
    dynamic_update_slice x29, local copies, waits for them, and re-layouts, place(): whole = lax.dynamic_update_slice(whole, part, (row, where * cols))  21.6 us
    pallas_call x5, Pallas kernels, per_head(): pl.pallas_call(kernel, out_shape=shapes, grid_spec=pltpu.PrefetchScalarGr...  20.6 us
    dot_general x4, matrix products, contract(): jnp.einsum('td,ti->di', left, right, preferred_element_type=F32)  18.6 us
  transfers between devices with their start and end apart: 60, of which 27 were waited for; matrix products, arithmetic and copies ran while one was open for 28% of the time, Pallas kernels for 16%

profile of v2, /device:TPU:0, one launch (start us, length us, event | category | flops | bytes accessed | tf_op | source)
XLA Modules:
  0.0 322.3 jit_solution(10814049040704522083)
XLA Ops:
  10.2 6.1 %collective-permute-done.1 = bf16[128,1024]{1,0:T(8,128)(2,1)S(1)} collective-permute-done((bf16[128,1024]{1,0:T(8,128)(2,1)S(1)}, bf16[128,1024]{1,0:T(8,128)(2,1)S(1)}, u32[]{:S(2)}, u32[]{:S(2)}) %collective-permute-start.1) | collective-permute-done | bytes 262176 | tf_op jit(solution)/shard_map/ppermute | solution.py:31
  32.8 8.7 %collective-permute-done.12 = bf16[128,1024]{1,0:T(8,128)(2,1)S(1)} collective-permute-done((bf16[128,1024]{1,0:T(8,128)(2,1)S(1)}, bf16[128,1024]{1,0:T(8,128)(2,1)S(1)}, u32[]{:S(2)}, u32[]{:S(2)}) %collective-permute-start.12) | collective-permute-done | bytes 262176 | tf_op jit(solution)/shard_map/ppermute | solution.py:35
  54.2 4.1 %collective-permute-done.14 = bf16[128,1024]{1,0:T(8,128)(2,1)S(1)} collective-permute-done((bf16[128,1024]{1,0:T(8,128)(2,1)S(1)}, bf16[128,1024]{1,0:T(8,128)(2,1)S(1)}, u32[]{:S(2)}, u32[]{:S(2)}) %collective-permute-start.14) | collective-permute-done | bytes 262176 | tf_op jit(solution)/shard_map/ppermute | solution.py:35
  67.7 8.2 %fusion.34.q_ref = f32[256,512]{1,0:T(8,128)} fusion(bf16[256,8192]{1,0:T(8,128)(2,1)} %constant_dynamic-update-slice_fusion.24, bf16[8192,512]{1,0:T(8,128)(2,1)} %wq_ref.15), kind=kOutput, calls=%fused_computation.95 | convolution fusion | flops 2147483648 | bytes 13107200 | tf_op jit(solution)/shard_map/dot_general | solution.py:249
  78.2 5.3 %fusion.35.k_ref = f32[256,512]{1,0:T(8,128)} fusion(bf16[256,8192]{1,0:T(8,128)(2,1)} %constant_dynamic-update-slice_fusion.24, bf16[8192,512]{1,0:T(8,128)(2,1)S(1)} %bitcast.27), kind=kOutput, calls=%fused_computation.96 | convolution fusion | flops 2147483648 | bytes 13107200 | tf_op jit(solution)/shard_map/dot_general | solution.py:250
  89.2 5.4 %collective-permute-done.7 = bf16[160,1024]{1,0:T(8,128)(2,1)S(1)} collective-permute-done((bf16[160,1024]{1,0:T(8,128)(2,1)S(1)}, bf16[160,1024]{1,0:T(8,128)(2,1)S(1)}, u32[]{:S(2)}, u32[]{:S(2)}) %collective-permute-start.7) | collective-permute-done | bytes 327712 | tf_op jit(solution)/shard_map/ppermute | solution.py:35
  96.4 5.3 %fusion.36.v_ref = f32[256,512]{1,0:T(8,128)} fusion(bf16[256,8192]{1,0:T(8,128)(2,1)} %constant_dynamic-update-slice_fusion.24, bf16[8192,512]{1,0:T(8,128)(2,1)S(1)} %bitcast.29), kind=kOutput, calls=%fused_computation.97 | convolution fusion | flops 2147483648 | bytes 13107200 | tf_op jit(solution)/shard_map/dot_general | solution.py:251
  101.7 4.1 %shard_map.101 = (bf16[256,512]{1,0:T(8,128)(2,1)}, bf16[256,512]{1,0:T(8,128)(2,1)}, bf16[256,512]{1,0:T(8,128)(2,1)}, bf16[1024,256]{1,0:T(8,128)(2,1)}, f32[256,512]{1,0:T(8,128)}, /*index=5*/bf16[512,128]{1,0:T(8,128)(2,1)}) custom-call(f32[256,512]{1,0:T(8,128)} %fusion.34.q_ref, f32[256,512]{1,0:T(8,128)} %fusion.35.k_ref, f32[256,512]{1,0:T(8,128)} %fusion.36.v_ref), custom_call_target="tpu_custom_call" | custom-call | flops 134217728 | bytes 3538944 | tf_op jit(solution)/shard_map/pallas_call | solution.py:119
  108.1 3.9 %constant_dynamic-slice_fusion.3 = (bf16[256,2048]{1,0:T(8,128)(2,1)}, bf16[256,2048]{1,0:T(8,128)(2,1)}, bf16[256,2048]{1,0:T(8,128)(2,1)}, bf16[256,2048]{1,0:T(8,128)(2,1)S(1)}) fusion(bf16[256,8192]{1,0:T(8,128)(2,1)} %constant_dynamic-update-slice_fusion.24, s32[]{:T(128)S(6)} %select_n.282, s32[]{:T(128)S(6)} %select_n.281, s32[]{:T(128)S(6)} %select_n.280, ...), kind=kLoop, calls=%fused_computation.58 | loop fusion | bytes 8388624 | tf_op jit(solution)/shard_map/dynamic_slice | solution.py:80
  116.2 4.0 %shard_map.102 = (f32[256,512]{1,0:T(8,128)}, f32[256,512]{1,0:T(8,128)}, bf16[256,512]{1,0:T(8,128)(2,1)}, bf16[512,128]{1,0:T(8,128)(2,1)}) custom-call(s32[1]{0:T(128)} %bitcast.1.c_ref, f32[256,512]{1,0:T(8,128)} %get-tuple-element.46.in_ref, bf16[256,512]{1,0:T(8,128)(2,1)} %get-tuple-element.47.qf_ref, bf16[512,128]{1,0:T(8,128)(2,1)} %copy-done.17, ...), custom_call_target="tpu_custom_call" | custom-call | flops 33554432 | bytes 2621440 | tf_op jit(solution)/shard_map/pallas_call | solution.py:119
  122.5 5.4 %collective-permute-done.9 = bf16[96,2048]{1,0:T(8,128)(2,1)S(1)} collective-permute-done((bf16[96,2048]{1,0:T(8,128)(2,1)S(1)}, bf16[96,2048]{1,0:T(8,128)(2,1)S(1)}, u32[]{:S(2)}, u32[]{:S(2)}) %collective-permute-start.9) | collective-permute-done | bytes 393248 | tf_op jit(solution)/shard_map/ppermute | solution.py:31
  129.3 10.9 %collective-permute-done.10 = bf16[96,2048]{1,0:T(8,128)(2,1)S(1)} collective-permute-done((bf16[96,2048]{1,0:T(8,128)(2,1)S(1)}, bf16[96,2048]{1,0:T(8,128)(2,1)S(1)}, u32[]{:S(2)}, u32[]{:S(2)}) %collective-permute-start.10) | collective-permute-done | bytes 393248 | tf_op jit(solution)/shard_map/ppermute | solution.py:31
  141.7 7.8 %fusion.37.ga_ref = f32[256,512]{1,0:T(8,128)} fusion(bf16[256,8192]{1,0:T(8,128)(2,1)} %slice_dynamic-update-slice_fusion.2, bf16[8192,512]{1,0:T(8,128)(2,1)} %param.11), kind=kOutput, calls=%fused_computation.98 | convolution fusion | flops 2147483648 | bytes 13107200 | tf_op jit(solution)/shard_map/dot_general | solution.py:278
  164.8 3.9 %constant_dynamic-slice_fusion.2 = (bf16[256,2048]{1,0:T(8,128)(2,1)S(1)}, bf16[256,2048]{1,0:T(8,128)(2,1)}, bf16[256,2048]{1,0:T(8,128)(2,1)}, bf16[256,2048]{1,0:T(8,128)(2,1)S(1)}) fusion(bf16[256,8192]{1,0:T(8,128)(2,1)} %slice_dynamic-update-slice_fusion, s32[]{:T(128)S(6)} %select_n.279, s32[]{:T(128)S(6)} %select_n.282, s32[]{:T(128)S(6)} %select_n.281, ...), kind=kLoop, calls=%fused_computation.57 | loop fusion | bytes 8388624 | tf_op jit(solution)/shard_map/dynamic_slice | solution.py:80
  168.8 4.6 %shard_map.104 = (bf16[256,512]{1,0:T(8,128)(2,1)}, f32[256,512]{1,0:T(8,128)}, f32[256,512]{1,0:T(8,128)}) custom-call(bf16[256,512]{1,0:T(8,128)(2,1)} %get-tuple-element.53.od_ref, bf16[256,512]{1,0:T(8,128)(2,1)} %get-tuple-element.47.qf_ref, bf16[256,512]{1,0:T(8,128)(2,1)} %get-tuple-element.54.kf_ref, bf16[256,512]{1,0:T(8,128)(2,1)} %get-tuple-element.55.vf_ref, ...), custom_call_target="tpu_custom_call" | custom-call | flops 268435456 | bytes 3538944 | tf_op jit(solution)/shard_map/pallas_call | solution.py:119
  175.2 4.0 %shard_map.105.kv_ref = bf16[2,256,512]{2,1,0:T(8,128)(2,1)} custom-call(s32[1]{0:T(128)} %bitcast.1.c_ref, f32[256,512]{1,0:T(8,128)} %get-tuple-element.59.fk_ref, f32[256,512]{1,0:T(8,128)} %get-tuple-element.60.fv_ref, bf16[256,512]{1,0:T(8,128)(2,1)} %get-tuple-element.54.kf_ref, bf16[256,512]{1,0:T(8,128)(2,1)} %get-tuple-element.55.vf_ref, ...), custom_call_target="tpu_custom_call" | custom-call | flops 67108864 | bytes 3014656 | tf_op jit(solution)/shard_map/pallas_call | solution.py:119
  223.1 6.3 %convolution_convert_fusion.2 = bf16[2048,512]{1,0:T(8,128)(2,1)} fusion(bf16[1024,2048]{1,0:T(8,128)(2,1)} %constant_dynamic-update-slice_fusion, bf16[256,512]{1,0:T(8,128)(2,1)} %collective-permute-done.50, bf16[256,512]{1,0:T(8,128)(2,1)S(1)} %collective-permute-done.49, bf16[256,512]{1,0:T(8,128)(2,1)} %collective-permute-done.48, ...), kind=kOutput, calls=%fused_computation.11 | convolution fusion | flops 2152726528 | bytes 7340032 | tf_op jit(solution)/shard_map/td,ti->di/dot_general | solution.py:337
  230.4 4.4 %collective-permute-done.37 = bf16[128,1024]{1,0:T(8,128)(2,1)S(1)} collective-permute-done((bf16[128,1024]{1,0:T(8,128)(2,1)S(1)}, bf16[128,1024]{1,0:T(8,128)(2,1)S(1)}, u32[]{:S(2)}, u32[]{:S(2)}) %collective-permute-start.37) | collective-permute-done | bytes 262176 | tf_op jit(solution)/shard_map/ppermute | solution.py:35
  238.1 6.5 %collective-permute-done.53 = bf16[2,256,512]{2,1,0:T(8,128)(2,1)S(1)} collective-permute-done((bf16[2,256,512]{2,1,0:T(8,128)(2,1)S(1)}, bf16[2,256,512]{2,1,0:T(8,128)(2,1)S(1)}, u32[]{:S(2)}, u32[]{:S(2)}) %collective-permute-start.53) | collective-permute-done | bytes 524320 | tf_op jit(solution)/shard_map/ppermute | solution.py:38
  257.6 5.0 %collective-permute-done.35 = bf16[128,1024]{1,0:T(8,128)(2,1)S(1)} collective-permute-done((bf16[128,1024]{1,0:T(8,128)(2,1)S(1)}, bf16[128,1024]{1,0:T(8,128)(2,1)S(1)}, u32[]{:S(2)}, u32[]{:S(2)}) %collective-permute-start.35) | collective-permute-done | bytes 262176 | tf_op jit(solution)/shard_map/ppermute | solution.py:35
  268.1 4.4 %collective-permute-done.39 = bf16[128,1024]{1,0:T(8,128)(2,1)S(1)} collective-permute-done((bf16[128,1024]{1,0:T(8,128)(2,1)S(1)}, bf16[128,1024]{1,0:T(8,128)(2,1)S(1)}, u32[]{:S(2)}, u32[]{:S(2)}) %collective-permute-start.39) | collective-permute-done | bytes 262176 | tf_op jit(solution)/shard_map/ppermute | solution.py:31
  272.8 31.4 %collective-permute-done.58 = bf16[256,512]{1,0:T(8,128)(2,1)S(1)} collective-permute-done((bf16[256,512]{1,0:T(8,128)(2,1)S(1)}, bf16[256,512]{1,0:T(8,128)(2,1)S(1)}, u32[]{:S(2)}, u32[]{:S(2)}) %collective-permute-start.58) | collective-permute-done | bytes 262176 | tf_op jit(solution)/shard_map/ppermute | solution.py:38
  308.5 4.8 %fusion.8 = bf16[2048,512]{1,0:T(8,128)(2,1)} fusion(bf16[256,2048]{1,0:T(8,128)(2,1)S(1)} %collective-permute-done.56, bf16[256,2048]{1,0:T(8,128)(2,1)S(1)} %collective-permute-done.55, bf16[256,2048]{1,0:T(8,128)(2,1)S(1)} %collective-permute-done.54, bf16[256,2048]{1,0:T(8,128)(2,1)S(1)} %get-tuple-element.83, ...), kind=kOutput, calls=%fused_computation.8 | convolution fusion | flops 2169503744 | bytes 7340032 | tf_op jit(solution)/shard_map/td,ti->di/dot_general | solution.py:337
  313.3 3.9 %collective-permute-done.47 = bf16[128,1024]{1,0:T(8,128)(2,1)S(1)} collective-permute-done((bf16[128,1024]{1,0:T(8,128)(2,1)S(1)}, bf16[128,1024]{1,0:T(8,128)(2,1)S(1)}, u32[]{:S(2)}, u32[]{:S(2)}) %collective-permute-start.47) | collective-permute-done | bytes 262176 | tf_op jit(solution)/shard_map/ppermute | solution.py:31
  (244 shorter events, 162.7 us)
Async XLA Ops:
  21.4 40.3 %collective-permute-start.15 = (bf16[128,1024]{1,0:T(8,128)(2,1)S(1)}, bf16[128,1024]{1,0:T(8,128)(2,1)S(1)}, u32[]{:S(2)}, u32[]{:S(2)}) collective-permute-start(bf16[128,1024]{1,0:T(8,128)(2,1)S(1)} %get-tuple-element.91), channel_id=1, source_target_pairs={{0,1},{1,0},{2,3},{3,2},{4,5},{5,4},{6,7},{7,6},{8,9},{9,8},{10,11... | collective-permute-start | bytes 786440 | tf_op jit(solution)/shard_map/ppermute | solution.py:35
  21.7 19.9 %collective-permute-start.12 = (bf16[128,1024]{1,0:T(8,128)(2,1)S(1)}, bf16[128,1024]{1,0:T(8,128)(2,1)S(1)}, u32[]{:S(2)}, u32[]{:S(2)}) collective-permute-start(bf16[128,1024]{1,0:T(8,128)(2,1)S(1)} %collective-permute-done.1), channel_id=1, source_target_pairs={{0,1},{1,0},{2,3},{3,2},{4,5},{5,4},{6,7},{7,6},{8,9},{9,8},{10,11... | collective-permute-start | bytes 786440 | tf_op jit(solution)/shard_map/ppermute | solution.py:35
  23.4 19.9 %collective-permute-start.18 = (bf16[128,1024]{1,0:T(8,128)(2,1)S(1)}, bf16[128,1024]{1,0:T(8,128)(2,1)S(1)}, u32[]{:S(2)}, u32[]{:S(2)}) collective-permute-start(bf16[128,1024]{1,0:T(8,128)(2,1)S(1)} %collective-permute-done.16), channel_id=1, source_target_pairs={{0,2},{1,3},{2,4},{3,5},{4,6},{5,7},{6,0},{7,1},{8,10},{9,11},{10,... | collective-permute-start | bytes 786440 | tf_op jit(solution)/shard_map/ppermute | solution.py:31
  27.4 17.9 %collective-permute-start.3 = (bf16[128,1024]{1,0:T(8,128)(2,1)S(1)}, bf16[128,1024]{1,0:T(8,128)(2,1)S(1)}, u32[]{:S(2)}, u32[]{:S(2)}) collective-permute-start(bf16[128,1024]{1,0:T(8,128)(2,1)S(1)} %collective-permute-done.2), channel_id=1, source_target_pairs={{0,2},{1,3},{2,4},{3,5},{4,6},{5,7},{6,0},{7,1},{8,10},{9,11},{10,... | collective-permute-start | bytes 786440 | tf_op jit(solution)/shard_map/ppermute | solution.py:31
  30.3 16.9 %collective-permute-start.13 = (bf16[128,1024]{1,0:T(8,128)(2,1)S(1)}, bf16[128,1024]{1,0:T(8,128)(2,1)S(1)}, u32[]{:S(2)}, u32[]{:S(2)}) collective-permute-start(bf16[128,1024]{1,0:T(8,128)(2,1)S(1)} %collective-permute-done.2), channel_id=1, source_target_pairs={{0,1},{1,0},{2,3},{3,2},{4,5},{5,4},{6,7},{7,6},{8,9},{9,8},{10,11... | collective-permute-start | bytes 786440 | tf_op jit(solution)/shard_map/ppermute | solution.py:35
  41.5 21.6 %collective-permute-start.17 = (bf16[128,1024]{1,0:T(8,128)(2,1)S(1)}, bf16[128,1024]{1,0:T(8,128)(2,1)S(1)}, u32[]{:S(2)}, u32[]{:S(2)}) collective-permute-start(bf16[128,1024]{1,0:T(8,128)(2,1)S(1)} %collective-permute-done.16), channel_id=1, source_target_pairs={{0,1},{1,0},{2,3},{3,2},{4,5},{5,4},{6,7},{7,6},{8,9},{9,8},{10,11... | collective-permute-start | bytes 786440 | tf_op jit(solution)/shard_map/ppermute | solution.py:35
  47.1 17.5 %collective-permute-start.19 = (bf16[128,1024]{1,0:T(8,128)(2,1)S(1)}, bf16[128,1024]{1,0:T(8,128)(2,1)S(1)}, u32[]{:S(2)}, u32[]{:S(2)}) collective-permute-start(bf16[128,1024]{1,0:T(8,128)(2,1)S(1)} %collective-permute-done.18), channel_id=1, source_target_pairs={{0,1},{1,0},{2,3},{3,2},{4,5},{5,4},{6,7},{7,6},{8,9},{9,8},{10,11... | collective-permute-start | bytes 786440 | tf_op jit(solution)/shard_map/ppermute | solution.py:35
  54.2 21.7 %collective-permute-start.4 = (bf16[160,1024]{1,0:T(8,128)(2,1)S(1)}, bf16[160,1024]{1,0:T(8,128)(2,1)S(1)}, u32[]{:S(2)}, u32[]{:S(2)}) collective-permute-start(bf16[160,1024]{1,0:T(8,128)(2,1)S(1)} %get-tuple-element.44), channel_id=1, source_target_pairs={{0,2},{1,3},{2,4},{3,5},{4,6},{5,7},{6,0},{7,1},{8,10},{9,11},{10,... | collective-permute-start | bytes 983048 | tf_op jit(solution)/shard_map/ppermute | solution.py:31
  107.7 20.1 %collective-permute-start.9 = (bf16[96,2048]{1,0:T(8,128)(2,1)S(1)}, bf16[96,2048]{1,0:T(8,128)(2,1)S(1)}, u32[]{:S(2)}, u32[]{:S(2)}) collective-permute-start(bf16[96,2048]{1,0:T(8,128)(2,1)S(1)} %pad_maximum_fusion.1), channel_id=1, source_target_pairs={{0,2},{1,3},{2,4},{3,5},{4,6},{5,7},{6,0},{7,1},{8,10},{9,11},{10,... | collective-permute-start | bytes 1179656 | tf_op jit(solution)/shard_map/ppermute | solution.py:31
  112.1 67.1 %collective-permute-start.31 = (bf16[256,2048]{1,0:T(8,128)(2,1)}, bf16[256,2048]{1,0:T(8,128)(2,1)}, u32[]{:S(2)}, u32[]{:S(2)}) collective-permute-start(bf16[256,2048]{1,0:T(8,128)(2,1)} %get-tuple-element.89), channel_id=1, source_target_pairs={{0,8},{8,0},{16,24},{24,16},{1,9},{9,1},{17,25},{25,17},{2,10},{10... | collective-permute-start | bytes 3145736 | tf_op jit(solution)/shard_map/ppermute | solution.py:38
  112.4 67.7 %collective-permute-start.32 = (bf16[256,2048]{1,0:T(8,128)(2,1)}, bf16[256,2048]{1,0:T(8,128)(2,1)}, u32[]{:S(2)}, u32[]{:S(2)}) collective-permute-start(bf16[256,2048]{1,0:T(8,128)(2,1)} %get-tuple-element.88), channel_id=1, source_target_pairs={{0,16},{8,24},{16,0},{24,8},{1,17},{9,25},{17,1},{25,9},{2,18},{10... | collective-permute-start | bytes 3145736 | tf_op jit(solution)/shard_map/ppermute | solution.py:38
  114.3 65.9 %collective-permute-start.33 = (bf16[256,2048]{1,0:T(8,128)(2,1)}, bf16[256,2048]{1,0:T(8,128)(2,1)}, u32[]{:S(2)}, u32[]{:S(2)}) collective-permute-start(bf16[256,2048]{1,0:T(8,128)(2,1)} %get-tuple-element.87), channel_id=1, source_target_pairs={{0,24},{8,16},{16,8},{24,0},{1,25},{9,17},{17,9},{25,1},{2,26},{10... | collective-permute-start | bytes 3145736 | tf_op jit(solution)/shard_map/ppermute | solution.py:38
  120.2 30.0 %collective-permute-start.26 = (bf16[160,1024]{1,0:T(8,128)(2,1)S(1)}, bf16[160,1024]{1,0:T(8,128)(2,1)S(1)}, u32[]{:S(2)}, u32[]{:S(2)}) collective-permute-start(bf16[160,1024]{1,0:T(8,128)(2,1)S(1)} %collective-permute-done.25), channel_id=1, source_target_pairs={{0,1},{1,0},{2,3},{3,2},{4,5},{5,4},{6,7},{7,6},{8,9},{9,8},{10,11... | collective-permute-start | bytes 983048 | tf_op jit(solution)/shard_map/ppermute | solution.py:35
  173.4 82.9 %collective-permute-start.59 = (bf16[256,512]{1,0:T(8,128)(2,1)}, bf16[256,512]{1,0:T(8,128)(2,1)}, u32[]{:S(2)}, u32[]{:S(2)}) collective-permute-start(bf16[256,512]{1,0:T(8,128)(2,1)} %get-tuple-element.49), channel_id=1, source_target_pairs={{0,24},{8,16},{16,8},{24,0},{1,25},{9,17},{17,9},{25,1},{2,26},{10... | collective-permute-start | bytes 786440 | tf_op jit(solution)/shard_map/ppermute | solution.py:38
  174.0 45.8 %collective-permute-start.50 = (bf16[256,512]{1,0:T(8,128)(2,1)}, bf16[256,512]{1,0:T(8,128)(2,1)}, u32[]{:S(2)}, u32[]{:S(2)}) collective-permute-start(bf16[256,512]{1,0:T(8,128)(2,1)} %get-tuple-element.58.q_ref), channel_id=1, source_target_pairs={{0,24},{8,16},{16,8},{24,0},{1,25},{9,17},{17,9},{25,1},{2,26},{10... | collective-permute-start | bytes 786440 | tf_op jit(solution)/shard_map/ppermute | solution.py:38
  179.2 41.7 %collective-permute-start.49 = (bf16[256,512]{1,0:T(8,128)(2,1)}, bf16[256,512]{1,0:T(8,128)(2,1)S(1)}, u32[]{:S(2)}, u32[]{:S(2)}) collective-permute-start(bf16[256,512]{1,0:T(8,128)(2,1)} %get-tuple-element.58.q_ref), channel_id=1, source_target_pairs={{0,16},{8,24},{16,0},{24,8},{1,17},{9,25},{17,1},{25,9},{2,18},{10... | collective-permute-start | bytes 786440 | tf_op jit(solution)/shard_map/ppermute | solution.py:38
  180.1 42.3 %collective-permute-start.48 = (bf16[256,512]{1,0:T(8,128)(2,1)}, bf16[256,512]{1,0:T(8,128)(2,1)}, u32[]{:S(2)}, u32[]{:S(2)}) collective-permute-start(bf16[256,512]{1,0:T(8,128)(2,1)} %get-tuple-element.58.q_ref), channel_id=1, source_target_pairs={{0,8},{8,0},{16,24},{24,16},{1,9},{9,1},{17,25},{25,17},{2,10},{10... | collective-permute-start | bytes 786440 | tf_op jit(solution)/shard_map/ppermute | solution.py:38
  182.0 54.3 %collective-permute-start.51 = (bf16[2,256,512]{2,1,0:T(8,128)(2,1)}, bf16[2,256,512]{2,1,0:T(8,128)(2,1)}, u32[]{:S(2)}, u32[]{:S(2)}) collective-permute-start(bf16[2,256,512]{2,1,0:T(8,128)(2,1)} %shard_map.105.kv_ref), channel_id=1, source_target_pairs={{0,8},{8,0},{16,24},{24,16},{1,9},{9,1},{17,25},{25,17},{2,10},{10... | collective-permute-start | bytes 1572872 | tf_op jit(solution)/shard_map/ppermute | solution.py:38
  219.8 18.3 %collective-permute-start.52 = (bf16[2,256,512]{2,1,0:T(8,128)(2,1)S(1)}, bf16[2,256,512]{2,1,0:T(8,128)(2,1)S(1)}, u32[]{:S(2)}, u32[]{:S(2)}) collective-permute-start(bf16[2,256,512]{2,1,0:T(8,128)(2,1)S(1)} %copy-done), channel_id=1, source_target_pairs={{0,16},{8,24},{16,0},{24,8},{1,17},{9,25},{17,1},{25,9},{2,18},{10... | collective-permute-start | bytes 1572872 | tf_op jit(solution)/shard_map/ppermute | solution.py:38
  250.7 55.5 %collective-permute-start.56 = (bf16[256,2048]{1,0:T(8,128)(2,1)S(1)}, bf16[256,2048]{1,0:T(8,128)(2,1)S(1)}, u32[]{:S(2)}, u32[]{:S(2)}) collective-permute-start(bf16[256,2048]{1,0:T(8,128)(2,1)S(1)} %copy-done.4), channel_id=1, source_target_pairs={{0,24},{8,16},{16,8},{24,0},{1,25},{9,17},{17,9},{25,1},{2,26},{10... | collective-permute-start | bytes 3145736 | tf_op jit(solution)/shard_map/ppermute | solution.py:38
  255.0 51.3 %collective-permute-start.55 = (bf16[256,2048]{1,0:T(8,128)(2,1)S(1)}, bf16[256,2048]{1,0:T(8,128)(2,1)S(1)}, u32[]{:S(2)}, u32[]{:S(2)}) collective-permute-start(bf16[256,2048]{1,0:T(8,128)(2,1)S(1)} %copy-done.3), channel_id=1, source_target_pairs={{0,16},{8,24},{16,0},{24,8},{1,17},{9,25},{17,1},{25,9},{2,18},{10... | collective-permute-start | bytes 3145736 | tf_op jit(solution)/shard_map/ppermute | solution.py:38
  256.4 52.2 %collective-permute-start.54 = (bf16[256,2048]{1,0:T(8,128)(2,1)S(1)}, bf16[256,2048]{1,0:T(8,128)(2,1)S(1)}, u32[]{:S(2)}, u32[]{:S(2)}) collective-permute-start(bf16[256,2048]{1,0:T(8,128)(2,1)S(1)} %get-tuple-element.86), channel_id=1, source_target_pairs={{0,8},{8,0},{16,24},{24,16},{1,9},{9,1},{17,25},{25,17},{2,10},{10... | collective-permute-start | bytes 3145736 | tf_op jit(solution)/shard_map/ppermute | solution.py:38
  267.2 36.9 %collective-permute-start.58 = (bf16[256,512]{1,0:T(8,128)(2,1)S(1)}, bf16[256,512]{1,0:T(8,128)(2,1)S(1)}, u32[]{:S(2)}, u32[]{:S(2)}) collective-permute-start(bf16[256,512]{1,0:T(8,128)(2,1)S(1)} %copy-done.23), channel_id=1, source_target_pairs={{0,16},{8,24},{16,0},{24,8},{1,17},{9,25},{17,1},{25,9},{2,18},{10... | collective-permute-start | bytes 786440 | tf_op jit(solution)/shard_map/ppermute | solution.py:38
  272.6 33.1 %collective-permute-start.57 = (bf16[256,512]{1,0:T(8,128)(2,1)S(1)}, bf16[256,512]{1,0:T(8,128)(2,1)S(1)}, u32[]{:S(2)}, u32[]{:S(2)}) collective-permute-start(bf16[256,512]{1,0:T(8,128)(2,1)S(1)} %copy-done.23), channel_id=1, source_target_pairs={{0,8},{8,0},{16,24},{24,16},{1,9},{9,1},{17,25},{25,17},{2,10},{10... | collective-permute-start | bytes 786440 | tf_op jit(solution)/shard_map/ppermute | solution.py:38
  (71 other events, 810.2 us)

commit v3 on v2

v3 whole, which is shorter than its diff:
```python
import functools

import jax
import jax.numpy as jnp
from jax import lax
from jax.experimental import pallas as pl
from jax.experimental.pallas import tpu as pltpu
from jax.sharding import PartitionSpec as P

HD = 128
F32 = jnp.float32
BF16 = jnp.bfloat16


def tie(x, *others):
    return lax.optimization_barrier((x,) + others)[0]


class Lines:
    def __init__(self):
        self.nh = lax.axis_size("head")
        self.nc = lax.axis_size("ctx")
        self.Z = 4 if self.nh % 4 == 0 else 1
        self.Y = self.nh // self.Z
        here = lax.axis_index("head")
        self.c = lax.axis_index("ctx")
        self.z = here // self.Y
        self.y = here % self.Y

    def along_z(self, x):
        return lax.ppermute(x, "head", [(i, (i + self.Y) % self.nh) for i in range(self.nh)])

    def along_y(self, x):
        Y = self.Y
        return lax.ppermute(x, "head", [(i, i // Y * Y + (i + 1) % Y) for i in range(self.nh)])

    def swap_z(self, x):
        Y = self.Y
        return lax.ppermute(x, "head", [(i, (i // Y ^ 1) * Y + i % Y) for i in range(self.nh)])

    def across(self, x, j):
        return lax.ppermute(x, "ctx", [(i, i ^ j) for i in range(self.nc)])

    def shard(self, k, j):
        return ((self.z - k) % self.Z) * self.Y + (self.y - j) % self.Y


def gather_piece(at, x, z_first, after=()):
    parts = []
    if z_first:
        now = x
        for k in range(at.Z):
            if k:
                now = at.along_z(tie(now, *after) if after and k == 1 else now)
            side = now
            for j in range(at.Y):
                if j:
                    side = at.along_y(side)
                parts.append((k, at.shard(k, j), side))
        return parts
    sides = [x]
    for _ in range(at.Y - 1):
        sides.append(at.along_y(sides[-1]))
    now = jnp.concatenate(sides, axis=1)
    cols = x.shape[1]
    for k in range(at.Z):
        if k:
            now = at.along_z(tie(now, *after) if after and k == 1 else now)
        for j in range(at.Y):
            parts.append((k, at.shard(k, j), now[:, j * cols : (j + 1) * cols]))
    return parts


def place(whole, parts, row, cols):
    for _, where, part in parts:
        whole = lax.dynamic_update_slice(whole, part, (row, where * cols))
    return whole


def slices_out(at, whole, *after):
    width = whole.shape[1] // at.nc
    half = whole.shape[0] // 2
    out, far = [], []
    for j in range(at.nc):
        piece = lax.dynamic_slice_in_dim(whole, (at.c ^ j) * width, width, 1)
        if j < 2:
            out.append(at.across(tie(piece, *after), j) if j else piece)
            continue
        for part in (piece[:half], piece[half:]):
            far.append(at.across(tie(part, *after, *far[-1:]), j))
        out.extend(far[-2:])
    return out, far


def slices_shared(at, whole):
    width = whole.shape[1] // at.nc
    half = whole.shape[0] // 2
    mine = (at.z % 2) * half
    out, far = [], []
    for j in range(at.nc):
        start = (at.c ^ j) * width
        if j < 2 or at.Z % 2:
            piece = lax.dynamic_slice_in_dim(whole, start, width, 1)
            out.append(at.across(piece, j) if j else piece)
            continue
        piece = lax.dynamic_slice(whole, (mine, start), (half, width))
        piece = at.across(tie(piece, *far[-1:]) if far else piece, j)
        far.append(piece)
        other = at.swap_z(piece)
        both = jnp.zeros((2 * half, width), whole.dtype)
        both = lax.dynamic_update_slice(both, piece, (mine, 0))
        out.append(lax.dynamic_update_slice(both, other, (half - mine, 0)))
    return out, far


def blocks_out(at, x):
    have = {0: x}
    bit = at.nc // 2
    while bit:
        have.update({j | bit: at.across(v, bit) for j, v in list(have.items())})
        bit //= 2
    return [have[j] for j in range(at.nc)]


def mm(a, b, ca, cb):
    return lax.dot_general(a, b, (((ca,), (cb,)), ((), ())), preferred_element_type=F32)


def slope(values):
    return jnp.where(values > 0, 1.0, jnp.exp(jnp.minimum(values, 0.0)))


def feature(values):
    return jnp.where(values > 0, values + 1.0, jnp.exp(jnp.minimum(values, 0.0)))


def causal(values):
    rows = lax.broadcasted_iota(jnp.int32, values.shape, 0)
    cols = lax.broadcasted_iota(jnp.int32, values.shape, 1)
    return jnp.where(rows >= cols, values, 0.0)


def whole_call(kernel, ins, outs, scalars=()):
    vmem = pl.BlockSpec(memory_space=pltpu.VMEM)
    return pl.pallas_call(
        kernel,
        out_shape=[jax.ShapeDtypeStruct(s, d) for s, d in outs],
        in_specs=[pl.BlockSpec(memory_space=pltpu.SMEM)] * len(scalars) + [vmem] * len(ins),
        out_specs=[vmem] * len(outs),
        compiler_params=pltpu.CompilerParams(vmem_limit_bytes=32 * 1024 * 1024),
        cost_estimate=pl.CostEstimate(flops=1000, bytes_accessed=1000, transcendentals=0),
    )(*scalars, *ins)


def heads(array):
    return [slice(i * HD, (i + 1) * HD) for i in range(array.shape[1] // HD)]


def forward_kernel(*refs):
    qa_ref, ka_ref, va_ref, qb_ref, kb_ref, vb_ref, q_ref, k_ref = refs[:8]
    qf_ref, kf_ref, vf_ref, sc_ref, in_ref, kv_ref = refs[8:]
    for i, at in enumerate(heads(q_ref)):
        query_lin = qa_ref[:, at] + qb_ref[:, at]
        key_lin = ka_ref[:, at] + kb_ref[:, at]
        q_ref[:, at] = query_lin
        k_ref[:, at] = key_lin
        qf = feature(query_lin).astype(BF16)
        kf = feature(key_lin).astype(BF16)
        vf = (va_ref[:, at] + vb_ref[:, at]).astype(BF16)
        scores = causal(mm(qf, kf, 1, 1)).astype(BF16)
        qf_ref[:, at] = qf
        kf_ref[:, at] = kf
        vf_ref[:, at] = vf
        sc_ref[i] = scores
        in_ref[:, at] = mm(scores, vf, 1, 0)
        kv_ref[at, :] = mm(kf, vf, 0, 0).astype(BF16)


def state_sum(c, refs, at, later):
    total = jnp.zeros((HD, HD), F32)
    for j, ref in enumerate(refs):
        other = c ^ (j + 1)
        use = (other > c) if later else (other < c)
        total = total + jnp.where(use, ref[at, :].astype(F32), 0.0)
    return total.astype(BF16)


def norm_kernel(nc, c_ref, in_ref, qf_ref, *refs):
    kv, (no_ref, sl_ref, ar_ref, pf_ref) = refs[: nc - 1], refs[nc - 1 :]
    for at in heads(qf_ref):
        prefix = state_sum(c_ref[0], kv, at, False)
        attended = in_ref[:, at] + mm(qf_ref[:, at], prefix, 1, 0)
        scale = lax.rsqrt(jnp.mean(attended * attended, axis=1, keepdims=True) + 1e-06)
        normed = attended * scale
        no_ref[:, at] = normed
        sl_ref[:, at] = jnp.broadcast_to(scale, normed.shape)
        ar_ref[:, at] = normed.astype(BF16)
        pf_ref[at, :] = prefix


def delta_kernel(ga_ref, gb_ref, no_ref, sl_ref, qf_ref, od_ref, qg_ref):
    for at in heads(qf_ref):
        grad = ga_ref[:, at] + gb_ref[:, at]
        normed = no_ref[:, at]
        mean = jnp.mean(grad * normed, axis=1, keepdims=True)
        delta = (sl_ref[:, at] * (grad - normed * mean)).astype(BF16)
        od_ref[:, at] = delta
        qg_ref[at, :] = mm(qf_ref[:, at], delta, 0, 0).astype(BF16)


def inner_kernel(
    od_ref, qf_ref, kf_ref, vf_ref, sc_ref, pf_ref, q_ref, qp_ref, qt_ref, fk_ref, fv_ref
):
    for i, at in enumerate(heads(qf_ref)):
        delta = od_ref[:, at]
        score_grad = causal(mm(delta, vf_ref[:, at], 1, 1)).astype(BF16)
        feat_q = mm(score_grad, kf_ref[:, at], 1, 0) + mm(delta, pf_ref[at, :], 1, 1)
        pre = feat_q * slope(q_ref[:, at])
        qp_ref[:, at] = pre.astype(BF16)
        qt_ref[at, :] = pre.T.astype(BF16)
        fk_ref[:, at] = mm(score_grad, qf_ref[:, at], 0, 0)
        fv_ref[:, at] = mm(sc_ref[i], delta, 0, 0)


def outer_kernel(nc, c_ref, fk_ref, fv_ref, kf_ref, vf_ref, k_ref, *refs):
    qg, (kv_ref, kt_ref) = refs[: nc - 1], refs[nc - 1 :]
    for at in heads(kf_ref):
        suffix = state_sum(c_ref[0], qg, at, True)
        feat_k = fk_ref[:, at] + mm(vf_ref[:, at], suffix, 1, 1)
        feat_v = fv_ref[:, at] + mm(kf_ref[:, at], suffix, 1, 0)
        key_pre = feat_k * slope(k_ref[:, at])
        kv_ref[0, :, at] = key_pre.astype(BF16)
        kv_ref[1, :, at] = feat_v.astype(BF16)
        kt_ref[0, at, :] = key_pre.T.astype(BF16)
        kt_ref[1, at, :] = feat_v.T.astype(BF16)


def part_kernel(count, s_ref, q_ref, kv_ref, wq_ref, wk_ref, wv_ref, *out_refs):
    total = mm(wq_ref[...], q_ref[...], 1, 0)
    total = total + mm(wk_ref[...], kv_ref[0], 1, 0)
    total = total + mm(wv_ref[...], kv_ref[1], 1, 0)
    for n, out_ref in enumerate(out_refs):

        @pl.when(pl.program_id(0) // count == n)
        def _():
            out_ref[...] = total.astype(out_ref.dtype)


def parts_of(places, query_turned, kv_turned, weights, cols, dtype):
    width, rows = query_turned.shape
    tile = min(512, cols)
    count = cols // tile
    weight = pl.BlockSpec((tile, width), lambda i, s: (s[i // count] * count + i % count, 0))

    def out(n):
        return pl.BlockSpec((tile, rows), lambda i, s: (jnp.clip(i - n * count, 0, count - 1), 0))

    return pl.pallas_call(
        functools.partial(part_kernel, count),
        out_shape=[jax.ShapeDtypeStruct((cols, rows), dtype)] * len(places),
        grid_spec=pltpu.PrefetchScalarGridSpec(
            num_scalar_prefetch=1,
            grid=(len(places) * count,),
            in_specs=[
                pl.BlockSpec((width, rows), lambda i, s: (0, 0)),
                pl.BlockSpec((2, width, rows), lambda i, s: (0, 0, 0)),
                weight,
                weight,
                weight,
            ],
            out_specs=[out(n) for n in range(len(places))],
        ),
        compiler_params=pltpu.CompilerParams(vmem_limit_bytes=32 * 1024 * 1024),
        cost_estimate=pl.CostEstimate(flops=1000, bytes_accessed=1000, transcendentals=0),
    )(jnp.stack(places).astype(jnp.int32), query_turned, kv_turned, *weights)


def local(tokens, out_grad, w_query, w_key, w_value, w_output):
    at = Lines()
    length, cols = tokens.shape
    width = w_query.shape[1]
    number = width // HD
    half = length // 2
    own = jnp.reshape(at.c, (1,)).astype(jnp.int32)

    tokens_in = gather_piece(at, tokens, True)
    cut = length * 5 // 8
    grads_a = gather_piece(at, out_grad[:cut], True)
    grads_b = gather_piece(at, out_grad[cut:], False)

    def split(parts):
        return [p for p in parts if p[0] < at.Z - 1], [p for p in parts if p[0] == at.Z - 1]

    group = at.Y * cols
    start = ((at.z + 1) % at.Z) * group

    def last_dot(whole, w):
        return jnp.dot(
            lax.dynamic_slice_in_dim(whole, start, group, 1),
            lax.dynamic_slice_in_dim(w, start, group, 0),
            preferred_element_type=F32,
        )
    blank = jnp.zeros((length, cols * at.nh), BF16)
    early, late = split(tokens_in)
    most_tokens = place(blank, early, 0, cols)
    ready_tokens = tie(most_tokens, split(grads_a)[1][0][2], split(grads_b)[1][0][2])
    most_lin = [
        jnp.dot(ready_tokens, w, preferred_element_type=F32) for w in (w_query, w_key, w_value)
    ]
    whole_tokens = place(tie(ready_tokens, *most_lin), late, 0, cols)
    last_lin = [last_dot(whole_tokens, w) for w in (w_query, w_key, w_value)]
    token_slices, far = slices_shared(at, whole_tokens)

    columns = (length, width)
    square = (number * HD, HD)
    query_lin, key_lin, query_feat, key_feat, value_feat, scores, intra, local_kv = whole_call(
        forward_kernel,
        [*most_lin, tie(last_lin[0], *far[:1]), *last_lin[1:]],
        [(columns, F32)] * 2
        + [(columns, BF16)] * 3
        + [((number, length, length), BF16), (columns, F32), (square, BF16)],
    )
    before = [at.across(local_kv, j) for j in range(1, at.nc)]
    (early_a, late_a), (early_b, late_b) = split(grads_a), split(grads_b)
    most_grads = place(place(blank, early_a, 0, cols), early_b, cut, cols)
    grad_most = jnp.dot(most_grads, w_output, preferred_element_type=F32)
    normed, scale, attn_rows, prefix = whole_call(
        functools.partial(norm_kernel, at.nc),
        [tie(intra, *far[1:]), query_feat, *before],
        [(columns, F32), (columns, F32), (columns, BF16), (square, BF16)],
        (own,),
    )
    rows_all = blocks_out(at, attn_rows)

    whole_grads = place(tie(most_grads, grad_most), late_a, 0, cols)
    whole_grads = place(whole_grads, late_b, cut, cols)
    grad_last = last_dot(whole_grads, w_output)
    out_delta, local_qg = whole_call(
        delta_kernel,
        [grad_most, grad_last, normed, scale, query_feat],
        [(columns, BF16), (square, BF16)],
    )
    after = [at.across(local_qg, j) for j in range(1, at.nc)]
    query_pre, query_turned, inner_k, inner_v = whole_call(
        inner_kernel,
        [out_delta, query_feat, key_feat, value_feat, scores, prefix, query_lin],
        [(columns, BF16), ((width, length), BF16), (columns, F32), (columns, F32)],
    )
    query_all = blocks_out(at, query_pre)
    kv_pre, kv_turned = whole_call(
        functools.partial(outer_kernel, at.nc),
        [inner_k, inner_v, key_feat, value_feat, key_lin, *after],
        [((2, length, width), BF16), ((2, width, length), BF16)],
        (own,),
    )
    kv_all = blocks_out(at, kv_pre)
    far_pre = query_all[2:3] + kv_all[2:3]
    grad_slices, far = slices_out(at, whole_grads, kv_pre, *far_pre)

    weights = (w_query, w_key, w_value)

    def parts(j, dtype):
        places = [at.shard(k, j) for k in range(1, at.Z + 1)]
        return parts_of(places, query_turned, kv_turned, weights, cols, dtype)

    def halves(x):
        return [x[: cols // 2].astype(F32), x[cols // 2 :].astype(F32)]

    sides = None
    for j in range(1, at.Y):
        mine = parts(j, BF16 if j == 1 else F32)
        if sides is not None:
            mine = [(m + s.astype(F32)).astype(BF16) for m, s in zip(mine, sides)]
        sides = [at.along_y(m) for m in mine]
    mine = parts(at.Y, F32)
    total = None
    for k in range(1, at.Z + 1):
        held = halves(mine[k - 1])
        due = [f for i, f in enumerate(far) if i * at.Z // len(far) + 2 == k]
        due = due + far_pre if k == 1 else due
        if due:
            held = lax.optimization_barrier((*held, *due))[:2]
        if sides is not None:
            held = [h + s for h, s in zip(held, halves(sides[k - 1]))]
        if total is not None:
            held = [h + t.astype(F32) for h, t in zip(held, total)]
        total = [h.astype(BF16) for h in held]
        if k < at.Z:
            total = [at.along_z(t) for t in total]
        if k == max(at.Z - 2, 1):
            free = total
    total = lax.optimization_barrier((*total, *far))[:2]
    input_grad = jnp.concatenate(total, axis=0).T

    def contract(left, right):
        return jnp.einsum("td,ti->di", left, right, preferred_element_type=F32).astype(BF16)

    tokens_cat = tie(jnp.concatenate(token_slices, axis=0), *free)
    grad_query = contract(tokens_cat, jnp.concatenate(query_all, axis=0))
    kv_cat = jnp.concatenate(kv_all, axis=1)
    grad_key = contract(tokens_cat, kv_cat[0])
    grad_value = contract(tokens_cat, kv_cat[1])
    grad_output = contract(
        jnp.concatenate(grad_slices, axis=0), jnp.concatenate(rows_all, axis=0)
    )
    return (input_grad, grad_query, grad_key, grad_value, grad_output)


def solution(mesh):
    return jax.shard_map(
        local,
        mesh=mesh,
        in_specs=(P("ctx", "head"),) * 2 + (P(None, "head"),) * 4,
        out_specs=(P("ctx", "head"),) * 5,
        check_vma=False,
    )
```

time: 323 us -> 263 us (0.81)
  Pallas kernels: 50.7 us -> 19.6 us
  local copies, waits for them, and re-layouts: 47.1 us -> 32.9 us
  matrix products: 48.6 us -> 36 us
  starting transfers between devices: 51.8 us -> 47.3 us
    pallas_call x13 -> x7, Pallas kernels: 50.7 us -> 19.6 us  [the longest x2 16.1 us: parts_of(): pl.pallas_call(functools.partial(part_kernel, count), out_shape=[jax.Shap...]
    dynamic_update_slice x29 -> x22, local copies, waits for them, and re-layouts: 21.6 us -> 10.9 us  [place(): whole = lax.dynamic_update_slice(whole, part, (row, where * cols))]
    dot_general x4 -> x7, matrix products: 22.2 us -> 11.8 us  [the longest x3 7.05 us: local(): jnp.dot(ready_tokens, w, preferred_element_type=F32)]
    ppermute x21 -> x13, starting transfers between devices: 25 us -> 15.2 us  [along_y(): lax.ppermute(x, 'head', [(i, i // Y * Y + (i + 1) % Y) for i in range(sel...]
    ppermute x21 -> x13, waiting for transfers between devices: 34 us -> 43.4 us  [along_y(): lax.ppermute(x, 'head', [(i, i // Y * Y + (i + 1) % Y) for i in range(sel...]
    dynamic_slice x2 -> x1, local copies, waits for them, and re-layouts: 7.89 us -> 2.76 us  [slices_out(): piece = lax.dynamic_slice_in_dim(whole, (at.c ^ j) * width, width, 1)]
    ppermute x18 -> x15, waiting for transfers between devices: 49 us -> 44.1 us  [along_z(): lax.ppermute(x, 'head', [(i, (i + self.Y) % self.nh) for i in range(self....]
    ppermute x21 -> x23, waiting for transfers between devices: 38.4 us -> 35.6 us  [across(): return lax.ppermute(x, 'ctx', [(i, i ^ j) for i in range(self.nc)])]
  transfers between devices with their start and end apart: 60 -> 53, of which waited for: 27 -> 25; matrix products, arithmetic and copies ran while one was open for 28% -> 23% of each run, Pallas kernels for 16% -> 7%
where the time goes in v3:
time: 263 us
  waiting for transfers between devices  123 us (47%)
  starting transfers between devices  47.3 us (18%)
  matrix products  36 us (14%)
  local copies, waits for them, and re-layouts  32.9 us (13%)
  Pallas kernels  19.6 us (7%)
    ppermute x15, waiting for transfers between devices, along_z(): lax.ppermute(x, 'head', [(i, (i + self.Y) % self.nh) for i in range(self....  44.1 us
    ppermute x13, waiting for transfers between devices, along_y(): lax.ppermute(x, 'head', [(i, i // Y * Y + (i + 1) % Y) for i in range(sel...  43.4 us
    ppermute x23, waiting for transfers between devices, across(): return lax.ppermute(x, 'ctx', [(i, i ^ j) for i in range(self.nc)])  35.6 us
    ppermute x23, starting transfers between devices, across(): return lax.ppermute(x, 'ctx', [(i, i ^ j) for i in range(self.nc)])  17.2 us
    dot_general x4, matrix products, contract(): jnp.einsum('td,ti->di', left, right, preferred_element_type=F32)  17.2 us
    pallas_call x2, Pallas kernels, parts_of(): pl.pallas_call(functools.partial(part_kernel, count), out_shape=[jax.Shap...  16.1 us
    ppermute x13, starting transfers between devices, along_y(): lax.ppermute(x, 'head', [(i, i // Y * Y + (i + 1) % Y) for i in range(sel...  15.2 us
    ppermute x15, starting transfers between devices, along_z(): lax.ppermute(x, 'head', [(i, (i + self.Y) % self.nh) for i in range(self....  12.9 us
  transfers between devices with their start and end apart: 53, of which 25 were waited for; matrix products, arithmetic and copies ran while one was open for 23% of the time, Pallas kernels for 7%

profile of v3, /device:TPU:0, one launch (start us, length us, event | category | flops | bytes accessed | tf_op | source)
XLA Modules:
  0.0 262.8 jit_solution(15195648197892555741)
XLA Ops:
  4.0 3.0 %collective-permute-start.1 = (bf16[160,1024]{1,0:T(8,128)(2,1)S(1)}, bf16[160,1024]{1,0:T(8,128)(2,1)S(1)}, u32[]{:S(2)}, u32[]{:S(2)}) collective-permute-start(bf16[160,1024]{1,0:T(8,128)(2,1)S(1)} %get-tuple-element.138), channel_id=1, source_target_pairs={{0,2},{1,3},{2,4},{3,5},{4,6},{5,7},{6,0},{7,1},{8,10},{9,11},{10,... | collective-permute-start | bytes 983048 | tf_op jit(solution)/shard_map/ppermute | solution.py:31
  11.3 6.4 %collective-permute-done.1 = bf16[160,1024]{1,0:T(8,128)(2,1)S(1)} collective-permute-done((bf16[160,1024]{1,0:T(8,128)(2,1)S(1)}, bf16[160,1024]{1,0:T(8,128)(2,1)S(1)}, u32[]{:S(2)}, u32[]{:S(2)}) %collective-permute-start.1) | collective-permute-done | bytes 327712 | tf_op jit(solution)/shard_map/ppermute | solution.py:31
  21.0 7.9 %collective-permute-done.12 = bf16[256,1024]{1,0:T(8,128)(2,1)S(1)} collective-permute-done((bf16[256,1024]{1,0:T(8,128)(2,1)S(1)}, bf16[256,1024]{1,0:T(8,128)(2,1)S(1)}, u32[]{:S(2)}, u32[]{:S(2)}) %collective-permute-start.12) | collective-permute-done | bytes 524320 | tf_op jit(solution)/shard_map/ppermute | solution.py:31
  30.7 5.2 %collective-permute-done.3 = bf16[160,1024]{1,0:T(8,128)(2,1)S(1)} collective-permute-done((bf16[160,1024]{1,0:T(8,128)(2,1)S(1)}, bf16[160,1024]{1,0:T(8,128)(2,1)S(1)}, u32[]{:S(2)}, u32[]{:S(2)}) %collective-permute-start.3) | collective-permute-done | bytes 327712 | tf_op jit(solution)/shard_map/ppermute | solution.py:31
  39.4 13.4 %collective-permute-done.4 = bf16[160,1024]{1,0:T(8,128)(2,1)S(1)} collective-permute-done((bf16[160,1024]{1,0:T(8,128)(2,1)S(1)}, bf16[160,1024]{1,0:T(8,128)(2,1)S(1)}, u32[]{:S(2)}, u32[]{:S(2)}) %collective-permute-start.4) | collective-permute-done | bytes 327712 | tf_op jit(solution)/shard_map/ppermute | solution.py:35
  64.5 13.6 %collective-permute-done.15 = bf16[256,1024]{1,0:T(8,128)(2,1)S(1)} collective-permute-done((bf16[256,1024]{1,0:T(8,128)(2,1)S(1)}, bf16[256,1024]{1,0:T(8,128)(2,1)S(1)}, u32[]{:S(2)}, u32[]{:S(2)}) %collective-permute-start.15) | collective-permute-done | bytes 524320 | tf_op jit(solution)/shard_map/ppermute | solution.py:35
  91.1 7.2 %collective-permute-done.7 = bf16[96,2048]{1,0:T(8,128)(2,1)S(1)} collective-permute-done((bf16[96,2048]{1,0:T(8,128)(2,1)S(1)}, bf16[96,2048]{1,0:T(8,128)(2,1)S(1)}, u32[]{:S(2)}, u32[]{:S(2)}) %collective-permute-start.7) | collective-permute-done | bytes 393248 | tf_op jit(solution)/shard_map/ppermute | solution.py:31
  99.7 7.0 %fusion.40.ga_ref = f32[256,512]{1,0:T(8,128)S(1)} fusion(bf16[256,8192]{1,0:T(8,128)(2,1)} %slice_dynamic-update-slice_fusion.1, bf16[8192,512]{1,0:T(8,128)(2,1)} %param.11), kind=kOutput, calls=%fused_computation.102 | convolution fusion | flops 2147483648 | bytes 13107200 | tf_op jit(solution)/shard_map/dot_general | solution.py:326
  113.5 3.0 %collective-permute-done.10 = bf16[96,2048]{1,0:T(8,128)(2,1)S(1)} collective-permute-done((bf16[96,2048]{1,0:T(8,128)(2,1)S(1)}, bf16[96,2048]{1,0:T(8,128)(2,1)S(1)}, u32[]{:S(2)}, u32[]{:S(2)}) %collective-permute-start.10) | collective-permute-done | bytes 393248 | tf_op jit(solution)/shard_map/ppermute | solution.py:31
  118.0 2.8 %constant_dynamic-slice_fusion = (bf16[256,2048]{1,0:T(8,128)(2,1)S(1)}, bf16[1024,2048]{1,0:T(8,128)(2,1)}) fusion(bf16[256,8192]{1,0:T(8,128)(2,1)} %slice_dynamic-update-slice_fusion, s32[]{:T(128)S(6)} %select_n.264, s32[]{:T(128)S(6)} %select_n.263), kind=kLoop, calls=%fused_computation.58 | loop fusion | bytes 4194312 | tf_op jit(solution)/shard_map/dynamic_slice | solution.py:85
  120.7 2.7 %fusion.32 = (bf16[128,2048]{1,0:T(8,128)(2,1)S(1)}, bf16[128,2048]{1,0:T(8,128)(2,1)}, bf16[128,2048]{1,0:T(8,128)(2,1)S(1)}, bf16[128,2048]{1,0:T(8,128)(2,1)}) fusion(bf16[256,8192]{1,0:T(8,128)(2,1)} %slice_dynamic-update-slice_fusion, s32[]{:T(128)S(6)} %add.337, s32[]{:T(128)S(6)} %select_n.262, s32[]{:T(128)S(6)} %select_n.261), kind=kLoop, calls=%fused_computation.94 | loop fusion | bytes 4194316 | tf_op jit(solution)/shard_map/slice | solution.py:89
  130.9 4.1 %collective-permute-done.19 = bf16[128,2048]{1,0:T(8,128)(2,1)} collective-permute-done((bf16[128,2048]{1,0:T(8,128)(2,1)S(1)}, bf16[128,2048]{1,0:T(8,128)(2,1)}, u32[]{:S(2)}, u32[]{:S(2)}) %collective-permute-start.19) | collective-permute-done | bytes 524320 | tf_op jit(solution)/shard_map/ppermute | solution.py:42
  150.1 8.1 %shard_map.106 = (f32[1024,256]{1,0:T(8,128)S(1)}, f32[1024,256]{1,0:T(8,128)S(1)}, f32[1024,256]{1,0:T(8,128)S(1)}, f32[1024,256]{1,0:T(8,128)S(1)}) custom-call(s32[4]{0:T(128)S(1)} %get-tuple-element.140.s_ref, bf16[512,256]{1,0:T(8,128)(2,1)S(1)} %get-tuple-element.72.q_ref, bf16[2,512,256]{2,1,0:T(8,128)(2,1)S(1)} %get-tuple-element.77.kv_ref, ...), custom_call_target="tpu_custom_call" | custom-call | flops 1000 | bytes 1000 | tf_op jit(solution)/shard_map/pallas_call | solution.py:258
  159.1 8.1 %shard_map.107 = (bf16[1024,256]{1,0:T(8,128)(2,1)S(1)}, bf16[1024,256]{1,0:T(8,128)(2,1)S(1)}, bf16[1024,256]{1,0:T(8,128)(2,1)S(1)}, bf16[1024,256]{1,0:T(8,128)(2,1)S(1)}) custom-call(s32[4]{0:T(128)S(1)} %get-tuple-element.141.s_ref, bf16[512,256]{1,0:T(8,128)(2,1)S(1)} %get-tuple-element.72.q_ref, bf16[2,512,256]{2,1,0:T(8,128)(2,1)S(1)} %get-tuple-element.77.kv_ref, ...), custom_call_target="tpu_custom_call" | custom-call | flops 1000 | bytes 1000 | tf_op jit(solution)/shard_map/pallas_call | solution.py:258
  173.9 8.0 %collective-permute-done.34 = bf16[1024,256]{1,0:T(8,128)(2,1)S(1)} collective-permute-done((bf16[1024,256]{1,0:T(8,128)(2,1)S(1)}, bf16[1024,256]{1,0:T(8,128)(2,1)S(1)}, u32[]{:S(2)}, u32[]{:S(2)}) %collective-permute-start.34) | collective-permute-done | bytes 524320 | tf_op jit(solution)/shard_map/ppermute | solution.py:35
  187.1 5.8 %collective-permute-done.33 = bf16[1024,256]{1,0:T(8,128)(2,1)S(1)} collective-permute-done((bf16[1024,256]{1,0:T(8,128)(2,1)S(1)}, bf16[1024,256]{1,0:T(8,128)(2,1)S(1)}, u32[]{:S(2)}, u32[]{:S(2)}) %collective-permute-start.33) | collective-permute-done | bytes 524320 | tf_op jit(solution)/shard_map/ppermute | solution.py:35
  193.4 3.9 %collective-permute-done.35 = bf16[512,256]{1,0:T(8,128)(2,1)S(1)} collective-permute-done((bf16[512,256]{1,0:T(8,128)(2,1)S(1)}, bf16[512,256]{1,0:T(8,128)(2,1)S(1)}, u32[]{:S(2)}, u32[]{:S(2)}) %collective-permute-start.35) | collective-permute-done | bytes 262176 | tf_op jit(solution)/shard_map/ppermute | solution.py:31
  201.1 7.5 %collective-permute-done.39 = bf16[512,256]{1,0:T(8,128)(2,1)S(1)} collective-permute-done((bf16[512,256]{1,0:T(8,128)(2,1)S(1)}, bf16[512,256]{1,0:T(8,128)(2,1)S(1)}, u32[]{:S(2)}, u32[]{:S(2)}) %collective-permute-start.39) | collective-permute-done | bytes 262176 | tf_op jit(solution)/shard_map/ppermute | solution.py:31
  214.9 3.8 %convolution_convert_fusion.3 = bf16[2048,512]{1,0:T(8,128)(2,1)} fusion(bf16[1024,2048]{1,0:T(8,128)(2,1)S(1)} %pad_maximum_fusion, bf16[256,512]{1,0:T(8,128)(2,1)S(1)} %collective-permute-done.46, bf16[256,512]{1,0:T(8,128)(2,1)S(1)} %collective-permute-done.26, bf16[256,512]{1,0:T(8,128)(2,1)S(1)} %collective-permute-done.45, ...), kind=kOutput, calls=%fused_computation.4 | convolution fusion | flops 2152726528 | bytes 7340032 | tf_op jit(solution)/shard_map/td,ti->di/dot_general | solution.py:396
  218.7 3.8 %convolution_convert_fusion.2 = bf16[2048,512]{1,0:T(8,128)(2,1)} fusion(bf16[1024,2048]{1,0:T(8,128)(2,1)S(1)} %pad_maximum_fusion, bf16[2,1024,512]{2,1,0:T(8,128)(2,1)S(1)} %constant_dynamic-update-slice_fusion), kind=kOutput, calls=%fused_computation.3 | convolution fusion | flops 2148532224 | bytes 7340032 | tf_op jit(solution)/shard_map/td,ti->di/dot_general | solution.py:396
  222.4 3.8 %convolution_convert_fusion.1 = bf16[2048,512]{1,0:T(8,128)(2,1)} fusion(bf16[1024,2048]{1,0:T(8,128)(2,1)S(1)} %pad_maximum_fusion, bf16[2,1024,512]{2,1,0:T(8,128)(2,1)S(1)} %constant_dynamic-update-slice_fusion), kind=kOutput, calls=%fused_computation.2 | convolution fusion | flops 2148532224 | bytes 7340032 | tf_op jit(solution)/shard_map/td,ti->di/dot_general | solution.py:396
  230.8 10.6 %collective-permute-done.30 = bf16[128,2048]{1,0:T(8,128)(2,1)S(1)} collective-permute-done((bf16[128,2048]{1,0:T(8,128)(2,1)S(1)}, bf16[128,2048]{1,0:T(8,128)(2,1)S(1)}, u32[]{:S(2)}, u32[]{:S(2)}) %collective-permute-start.30) | collective-permute-done | bytes 524320 | tf_op jit(solution)/shard_map/ppermute | solution.py:42
  245.4 9.5 %collective-permute-done.41 = bf16[128,2048]{1,0:T(8,128)(2,1)S(1)} collective-permute-done((bf16[128,2048]{1,0:T(8,128)(2,1)S(1)}, bf16[128,2048]{1,0:T(8,128)(2,1)S(1)}, u32[]{:S(2)}, u32[]{:S(2)}) %collective-permute-start.41) | collective-permute-done | bytes 524320 | tf_op jit(solution)/shard_map/ppermute | solution.py:42
  256.9 5.9 %convolution_convert_fusion = bf16[2048,512]{1,0:T(8,128)(2,1)} fusion(bf16[1024,2048]{1,0:T(8,128)(2,1)} %constant_dynamic-update-slice_fusion.4, bf16[256,512]{1,0:T(8,128)(2,1)S(1)} %collective-permute-done.52, bf16[256,512]{1,0:T(8,128)(2,1)S(1)} %collective-permute-done.51, bf16[256,512]{1,0:T(8,128)(2,1)S(1)} %collective-permute-done.50, ...), kind=kOutput, calls=%fused_computation.1 | convolution fusion | flops 2152726528 | bytes 7340032 | tf_op jit(solution)/shard_map/td,ti->di/dot_general | solution.py:396
  (187 shorter events, 106.6 us)
Async XLA Ops:
  8.6 20.3 %collective-permute-start.12 = (bf16[256,1024]{1,0:T(8,128)(2,1)S(1)}, bf16[256,1024]{1,0:T(8,128)(2,1)S(1)}, u32[]{:S(2)}, u32[]{:S(2)}) collective-permute-start(bf16[256,1024]{1,0:T(8,128)(2,1)S(1)} %copy-done.3), channel_id=1, source_target_pairs={{0,2},{1,3},{2,4},{3,5},{4,6},{5,7},{6,0},{7,1},{8,10},{9,11},{10,... | collective-permute-start | bytes 1572872 | tf_op jit(solution)/shard_map/ppermute | solution.py:31
  10.2 20.5 %collective-permute-start.11 = (bf16[256,1024]{1,0:T(8,128)(2,1)S(1)}, bf16[256,1024]{1,0:T(8,128)(2,1)S(1)}, u32[]{:S(2)}, u32[]{:S(2)}) collective-permute-start(bf16[256,1024]{1,0:T(8,128)(2,1)S(1)} %copy-done.3), channel_id=1, source_target_pairs={{0,1},{1,0},{2,3},{3,2},{4,5},{5,4},{6,7},{7,6},{8,9},{9,8},{10,11... | collective-permute-start | bytes 1572872 | tf_op jit(solution)/shard_map/ppermute | solution.py:35
  17.7 20.1 %collective-permute-start.2 = (bf16[160,1024]{1,0:T(8,128)(2,1)S(1)}, bf16[160,1024]{1,0:T(8,128)(2,1)S(1)}, u32[]{:S(2)}, u32[]{:S(2)}) collective-permute-start(bf16[160,1024]{1,0:T(8,128)(2,1)S(1)} %collective-permute-done.1), channel_id=1, source_target_pairs={{0,1},{1,0},{2,3},{3,2},{4,5},{5,4},{6,7},{7,6},{8,9},{9,8},{10,11... | collective-permute-start | bytes 983048 | tf_op jit(solution)/shard_map/ppermute | solution.py:35
  19.4 16.5 %collective-permute-start.3 = (bf16[160,1024]{1,0:T(8,128)(2,1)S(1)}, bf16[160,1024]{1,0:T(8,128)(2,1)S(1)}, u32[]{:S(2)}, u32[]{:S(2)}) collective-permute-start(bf16[160,1024]{1,0:T(8,128)(2,1)S(1)} %collective-permute-done.1), channel_id=1, source_target_pairs={{0,2},{1,3},{2,4},{3,5},{4,6},{5,7},{6,0},{7,1},{8,10},{9,11},{10,... | collective-permute-start | bytes 983048 | tf_op jit(solution)/shard_map/ppermute | solution.py:31
  28.9 30.6 %collective-permute-start.13 = (bf16[256,1024]{1,0:T(8,128)(2,1)S(1)}, bf16[256,1024]{1,0:T(8,128)(2,1)S(1)}, u32[]{:S(2)}, u32[]{:S(2)}) collective-permute-start(bf16[256,1024]{1,0:T(8,128)(2,1)S(1)} %collective-permute-done.12), channel_id=1, source_target_pairs={{0,1},{1,0},{2,3},{3,2},{4,5},{5,4},{6,7},{7,6},{8,9},{9,8},{10,11... | collective-permute-start | bytes 1572872 | tf_op jit(solution)/shard_map/ppermute | solution.py:35
  30.7 25.7 %collective-permute-start.14 = (bf16[256,1024]{1,0:T(8,128)(2,1)S(1)}, bf16[256,1024]{1,0:T(8,128)(2,1)S(1)}, u32[]{:S(2)}, u32[]{:S(2)}) collective-permute-start(bf16[256,1024]{1,0:T(8,128)(2,1)S(1)} %collective-permute-done.12), channel_id=1, source_target_pairs={{0,2},{1,3},{2,4},{3,5},{4,6},{5,7},{6,0},{7,1},{8,10},{9,11},{10,... | collective-permute-start | bytes 1572872 | tf_op jit(solution)/shard_map/ppermute | solution.py:31
  35.9 16.9 %collective-permute-start.4 = (bf16[160,1024]{1,0:T(8,128)(2,1)S(1)}, bf16[160,1024]{1,0:T(8,128)(2,1)S(1)}, u32[]{:S(2)}, u32[]{:S(2)}) collective-permute-start(bf16[160,1024]{1,0:T(8,128)(2,1)S(1)} %collective-permute-done.3), channel_id=1, source_target_pairs={{0,1},{1,0},{2,3},{3,2},{4,5},{5,4},{6,7},{7,6},{8,9},{9,8},{10,11... | collective-permute-start | bytes 983048 | tf_op jit(solution)/shard_map/ppermute | solution.py:35
  37.7 18.0 %collective-permute-start.8 = (bf16[160,1024]{1,0:T(8,128)(2,1)S(1)}, bf16[160,1024]{1,0:T(8,128)(2,1)S(1)}, u32[]{:S(2)}, u32[]{:S(2)}) collective-permute-start(bf16[160,1024]{1,0:T(8,128)(2,1)S(1)} %collective-permute-done.3), channel_id=1, source_target_pairs={{0,2},{1,3},{2,4},{3,5},{4,6},{5,7},{6,0},{7,1},{8,10},{9,11},{10,... | collective-permute-start | bytes 983048 | tf_op jit(solution)/shard_map/ppermute | solution.py:31
  55.8 52.0 %collective-permute-start.9 = (bf16[160,1024]{1,0:T(8,128)(2,1)S(1)}, bf16[160,1024]{1,0:T(8,128)(2,1)S(1)}, u32[]{:S(2)}, u32[]{:S(2)}) collective-permute-start(bf16[160,1024]{1,0:T(8,128)(2,1)S(1)} %collective-permute-done.8), channel_id=1, source_target_pairs={{0,1},{1,0},{2,3},{3,2},{4,5},{5,4},{6,7},{7,6},{8,9},{9,8},{10,11... | collective-permute-start | bytes 983048 | tf_op jit(solution)/shard_map/ppermute | solution.py:35
  56.4 21.7 %collective-permute-start.15 = (bf16[256,1024]{1,0:T(8,128)(2,1)S(1)}, bf16[256,1024]{1,0:T(8,128)(2,1)S(1)}, u32[]{:S(2)}, u32[]{:S(2)}) collective-permute-start(bf16[256,1024]{1,0:T(8,128)(2,1)S(1)} %collective-permute-done.14), channel_id=1, source_target_pairs={{0,1},{1,0},{2,3},{3,2},{4,5},{5,4},{6,7},{7,6},{8,9},{9,8},{10,11... | collective-permute-start | bytes 1572872 | tf_op jit(solution)/shard_map/ppermute | solution.py:35
  57.8 28.7 %collective-permute-start.16 = (bf16[256,1024]{1,0:T(8,128)(2,1)S(1)}, bf16[256,1024]{1,0:T(8,128)(2,1)S(1)}, u32[]{:S(2)}, u32[]{:S(2)}) collective-permute-start(bf16[256,1024]{1,0:T(8,128)(2,1)S(1)} %collective-permute-done.14), channel_id=1, source_target_pairs={{0,2},{1,3},{2,4},{3,5},{4,6},{5,7},{6,0},{7,1},{8,10},{9,11},{10,... | collective-permute-start | bytes 1572872 | tf_op jit(solution)/shard_map/ppermute | solution.py:31
  62.2 25.8 %collective-permute-start.6 = (bf16[96,2048]{1,0:T(8,128)(2,1)S(1)}, bf16[96,2048]{1,0:T(8,128)(2,1)S(1)}, u32[]{:S(2)}, u32[]{:S(2)}) collective-permute-start(bf16[96,2048]{1,0:T(8,128)(2,1)S(1)} %pad_maximum_fusion.1), channel_id=1, source_target_pairs={{0,2},{1,3},{2,4},{3,5},{4,6},{5,7},{6,0},{7,1},{8,10},{9,11},{10,... | collective-permute-start | bytes 1179656 | tf_op jit(solution)/shard_map/ppermute | solution.py:31
  86.5 22.1 %collective-permute-start.17 = (bf16[256,1024]{1,0:T(8,128)(2,1)S(1)}, bf16[256,1024]{1,0:T(8,128)(2,1)S(1)}, u32[]{:S(2)}, u32[]{:S(2)}) collective-permute-start(bf16[256,1024]{1,0:T(8,128)(2,1)S(1)} %collective-permute-done.16), channel_id=1, source_target_pairs={{0,1},{1,0},{2,3},{3,2},{4,5},{5,4},{6,7},{7,6},{8,9},{9,8},{10,11... | collective-permute-start | bytes 1572872 | tf_op jit(solution)/shard_map/ppermute | solution.py:35
  123.5 22.4 %collective-permute-start.43 = (bf16[128,2048]{1,0:T(8,128)(2,1)S(1)}, bf16[128,2048]{1,0:T(8,128)(2,1)S(1)}, u32[]{:S(2)}, u32[]{:S(2)}) collective-permute-start(bf16[128,2048]{1,0:T(8,128)(2,1)S(1)} %collective-permute-done.18), channel_id=1, source_target_pairs={{0,2},{1,3},{2,0},{3,1},{4,6},{5,7},{6,4},{7,5},{8,10},{9,11},{10,... | collective-permute-start | bytes 1572872 | tf_op jit(solution)/shard_map/ppermute | solution.py:39
  135.0 48.1 %collective-permute-start.42 = (bf16[256,2048]{1,0:T(8,128)(2,1)}, bf16[256,2048]{1,0:T(8,128)(2,1)}, u32[]{:S(2)}, u32[]{:S(2)}) collective-permute-start(bf16[256,2048]{1,0:T(8,128)(2,1)} %get-tuple-element.113), channel_id=1, source_target_pairs={{0,8},{8,0},{16,24},{24,16},{1,9},{9,1},{17,25},{25,17},{2,10},{10... | collective-permute-start | bytes 3145736 | tf_op jit(solution)/shard_map/ppermute | solution.py:42
  145.9 23.7 %collective-permute-start.26 = (bf16[256,512]{1,0:T(8,128)(2,1)S(1)}, bf16[256,512]{1,0:T(8,128)(2,1)S(1)}, u32[]{:S(2)}, u32[]{:S(2)}) collective-permute-start(bf16[256,512]{1,0:T(8,128)(2,1)S(1)} %get-tuple-element.80), channel_id=1, source_target_pairs={{0,16},{8,24},{16,0},{24,8},{1,17},{9,25},{17,1},{25,9},{2,18},{10... | collective-permute-start | bytes 786440 | tf_op jit(solution)/shard_map/ppermute | solution.py:42
  146.7 21.5 %collective-permute-start.44 = (bf16[128,2048]{1,0:T(8,128)(2,1)}, bf16[128,2048]{1,0:T(8,128)(2,1)}, u32[]{:S(2)}, u32[]{:S(2)}) collective-permute-start(bf16[128,2048]{1,0:T(8,128)(2,1)} %collective-permute-done.19), channel_id=1, source_target_pairs={{0,2},{1,3},{2,0},{3,1},{4,6},{5,7},{6,4},{7,5},{8,10},{9,11},{10,... | collective-permute-start | bytes 1572872 | tf_op jit(solution)/shard_map/ppermute | solution.py:39
  168.2 29.4 %collective-permute-start.47 = (bf16[2,256,512]{2,1,0:T(8,128)(2,1)S(1)}, bf16[2,256,512]{2,1,0:T(8,128)(2,1)S(1)}, u32[]{:S(2)}, u32[]{:S(2)}) collective-permute-start(bf16[2,256,512]{2,1,0:T(8,128)(2,1)S(1)} %get-tuple-element.79), channel_id=1, source_target_pairs={{0,8},{8,0},{16,24},{24,16},{1,9},{9,1},{17,25},{25,17},{2,10},{10... | collective-permute-start | bytes 1572872 | tf_op jit(solution)/shard_map/ppermute | solution.py:42
  169.6 23.3 %collective-permute-start.33 = (bf16[1024,256]{1,0:T(8,128)(2,1)S(1)}, bf16[1024,256]{1,0:T(8,128)(2,1)S(1)}, u32[]{:S(2)}, u32[]{:S(2)}) collective-permute-start(bf16[1024,256]{1,0:T(8,128)(2,1)S(1)} %get-tuple-element.91), channel_id=1, source_target_pairs={{0,1},{1,0},{2,3},{3,2},{4,5},{5,4},{6,7},{7,6},{8,9},{9,8},{10,11... | collective-permute-start | bytes 1572872 | tf_op jit(solution)/shard_map/ppermute | solution.py:35
  187.1 25.1 %collective-permute-start.45 = (bf16[256,512]{1,0:T(8,128)(2,1)S(1)}, bf16[256,512]{1,0:T(8,128)(2,1)S(1)}, u32[]{:S(2)}, u32[]{:S(2)}) collective-permute-start(bf16[256,512]{1,0:T(8,128)(2,1)S(1)} %get-tuple-element.80), channel_id=1, source_target_pairs={{0,8},{8,0},{16,24},{24,16},{1,9},{9,1},{17,25},{25,17},{2,10},{10... | collective-permute-start | bytes 786440 | tf_op jit(solution)/shard_map/ppermute | solution.py:42
  192.9 19.4 %collective-permute-start.46 = (bf16[256,512]{1,0:T(8,128)(2,1)S(1)}, bf16[256,512]{1,0:T(8,128)(2,1)S(1)}, u32[]{:S(2)}, u32[]{:S(2)}) collective-permute-start(bf16[256,512]{1,0:T(8,128)(2,1)S(1)} %collective-permute-done.26), channel_id=1, source_target_pairs={{0,8},{8,0},{16,24},{24,16},{1,9},{9,1},{17,25},{25,17},{2,10},{10... | collective-permute-start | bytes 786440 | tf_op jit(solution)/shard_map/ppermute | solution.py:42
  199.0 45.5 %collective-permute-start.51 = (bf16[256,512]{1,0:T(8,128)(2,1)S(1)}, bf16[256,512]{1,0:T(8,128)(2,1)S(1)}, u32[]{:S(2)}, u32[]{:S(2)}) collective-permute-start(bf16[256,512]{1,0:T(8,128)(2,1)S(1)} %get-tuple-element.104), channel_id=1, source_target_pairs={{0,16},{8,24},{16,0},{24,8},{1,17},{9,25},{17,1},{25,9},{2,18},{10... | collective-permute-start | bytes 786440 | tf_op jit(solution)/shard_map/ppermute | solution.py:42
  208.6 19.8 %collective-permute-start.32 = (bf16[1024,256]{1,0:T(8,128)(2,1)S(1)}, bf16[1024,256]{1,0:T(8,128)(2,1)S(1)}, u32[]{:S(2)}, u32[]{:S(2)}) collective-permute-start(bf16[1024,256]{1,0:T(8,128)(2,1)S(1)} %get-tuple-element.88), channel_id=1, source_target_pairs={{0,1},{1,0},{2,3},{3,2},{4,5},{5,4},{6,7},{7,6},{8,9},{9,8},{10,11... | collective-permute-start | bytes 1572872 | tf_op jit(solution)/shard_map/ppermute | solution.py:35
  211.9 33.2 %collective-permute-start.31 = (bf16[1024,256]{1,0:T(8,128)(2,1)S(1)}, bf16[1024,256]{1,0:T(8,128)(2,1)S(1)}, u32[]{:S(2)}, u32[]{:S(2)}) collective-permute-start(bf16[1024,256]{1,0:T(8,128)(2,1)S(1)} %get-tuple-element.85), channel_id=1, source_target_pairs={{0,1},{1,0},{2,3},{3,2},{4,5},{5,4},{6,7},{7,6},{8,9},{9,8},{10,11... | collective-permute-start | bytes 1572872 | tf_op jit(solution)/shard_map/ppermute | solution.py:35
  (41 other events, 543.6 us)

commit v4 on v3

--- a/solution.py
+++ b/solution.py
@@ -51,8 +51,8 @@
         now = x
         for k in range(at.Z):
             if k:
-                now = at.along_z(tie(now, *after) if after and k == 1 else now)
-            side = now
+                now = at.along_z(now)
+            side = tie(now, *after) if k == at.Z - 1 else now
             for j in range(at.Y):
                 if j:
                     side = at.along_y(side)
@@ -65,7 +65,7 @@
     cols = x.shape[1]
     for k in range(at.Z):
         if k:
-            now = at.along_z(tie(now, *after) if after and k == 1 else now)
+            now = at.along_z(tie(now, *after) if k == at.Z - 1 else now)
         for j in range(at.Y):
             parts.append((k, at.shard(k, j), now[:, j * cols : (j + 1) * cols]))
     return parts
@@ -77,39 +77,27 @@
     return whole
 
 
-def slices_out(at, whole, *after):
+def slices_of(at, whole, shared, *after):
+    rows = whole.shape[0]
     width = whole.shape[1] // at.nc
-    half = whole.shape[0] // 2
-    out, far = [], []
-    for j in range(at.nc):
-        piece = lax.dynamic_slice_in_dim(whole, (at.c ^ j) * width, width, 1)
-        if j < 2:
-            out.append(at.across(tie(piece, *after), j) if j else piece)
-            continue
-        for part in (piece[:half], piece[half:]):
-            far.append(at.across(tie(part, *after, *far[-1:]), j))
-        out.extend(far[-2:])
-    return out, far
-
-
-def slices_shared(at, whole):
-    width = whole.shape[1] // at.nc
-    half = whole.shape[0] // 2
-    mine = (at.z % 2) * half
-    out, far = [], []
-    for j in range(at.nc):
-        start = (at.c ^ j) * width
-        if j < 2 or at.Z % 2:
-            piece = lax.dynamic_slice_in_dim(whole, start, width, 1)
-            out.append(at.across(piece, j) if j else piece)
-            continue
-        piece = lax.dynamic_slice(whole, (mine, start), (half, width))
-        piece = at.across(tie(piece, *far[-1:]) if far else piece, j)
-        far.append(piece)
-        other = at.swap_z(piece)
-        both = jnp.zeros((2 * half, width), whole.dtype)
-        both = lax.dynamic_update_slice(both, piece, (mine, 0))
-        out.append(lax.dynamic_update_slice(both, other, (half - mine, 0)))
+    shared = shared and at.Z % 2 == 0
+    half = rows // 2 if shared else rows
+    mine = (at.z % 2) * half if shared else 0
+
+    def piece(j, start, count):
+        return lax.dynamic_slice(whole, (start, (at.c ^ j) * width), (count, width))
+
+    out = [piece(0, 0, rows), at.across(tie(piece(1, 0, rows), *after), 1)]
+    far = []
+    for j in range(2, at.nc, 2):
+        both = jnp.stack([piece(j, mine, half), piece(j + 1, mine, half)])
+        both = at.across(tie(both, *after, *far[-1:]), j)
+        far.append(both)
+        if shared:
+            full = jnp.zeros((2, rows, width), whole.dtype)
+            full = lax.dynamic_update_slice(full, both, (0, mine, 0))
+            both = lax.dynamic_update_slice(full, at.swap_z(both), (0, half - mine, 0))
+        out += [both[0], at.across(both[1], 1)]
     return out, far
 
 
@@ -284,10 +272,6 @@
     own = jnp.reshape(at.c, (1,)).astype(jnp.int32)
 
     tokens_in = gather_piece(at, tokens, True)
-    cut = length * 5 // 8
-    grads_a = gather_piece(at, out_grad[:cut], True)
-    grads_b = gather_piece(at, out_grad[cut:], False)
-
     def split(parts):
         return [p for p in parts if p[0] < at.Z - 1], [p for p in parts if p[0] == at.Z - 1]
 
@@ -303,19 +287,21 @@
     blank = jnp.zeros((length, cols * at.nh), BF16)
     early, late = split(tokens_in)
     most_tokens = place(blank, early, 0, cols)
-    ready_tokens = tie(most_tokens, split(grads_a)[1][0][2], split(grads_b)[1][0][2])
     most_lin = [
-        jnp.dot(ready_tokens, w, preferred_element_type=F32) for w in (w_query, w_key, w_value)
+        jnp.dot(most_tokens, w, preferred_element_type=F32) for w in (w_query, w_key, w_value)
     ]
-    whole_tokens = place(tie(ready_tokens, *most_lin), late, 0, cols)
+    cut = length * 5 // 8
+    grads_a = gather_piece(at, out_grad[:cut], True, most_lin)
+    grads_b = gather_piece(at, out_grad[cut:], False, most_lin)
+    whole_tokens = place(tie(most_tokens, *most_lin), late, 0, cols)
     last_lin = [last_dot(whole_tokens, w) for w in (w_query, w_key, w_value)]
-    token_slices, far = slices_shared(at, whole_tokens)
+    token_slices, far = slices_of(at, whole_tokens, True)
 
     columns = (length, width)
     square = (number * HD, HD)
     query_lin, key_lin, query_feat, key_feat, value_feat, scores, intra, local_kv = whole_call(
         forward_kernel,
-        [*most_lin, tie(last_lin[0], *far[:1]), *last_lin[1:]],
+        [*most_lin, *last_lin],
         [(columns, F32)] * 2
         + [(columns, BF16)] * 3
         + [((number, length, length), BF16), (columns, F32), (square, BF16)],
@@ -323,10 +309,11 @@
     before = [at.across(local_kv, j) for j in range(1, at.nc)]
     (early_a, late_a), (early_b, late_b) = split(grads_a), split(grads_b)
     most_grads = place(place(blank, early_a, 0, cols), early_b, cut, cols)
+    most_grads = tie(most_grads, local_kv)
     grad_most = jnp.dot(most_grads, w_output, preferred_element_type=F32)
     normed, scale, attn_rows, prefix = whole_call(
         functools.partial(norm_kernel, at.nc),
-        [tie(intra, *far[1:]), query_feat, *before],
+        [intra, query_feat, *before],
         [(columns, F32), (columns, F32), (columns, BF16), (square, BF16)],
         (own,),
     )
@@ -337,7 +324,7 @@
     grad_last = last_dot(whole_grads, w_output)
     out_delta, local_qg = whole_call(
         delta_kernel,
-        [grad_most, grad_last, normed, scale, query_feat],
+        [tie(grad_most, *far), grad_last, normed, scale, query_feat],
         [(columns, BF16), (square, BF16)],
     )
     after = [at.across(local_qg, j) for j in range(1, at.nc)]
@@ -355,7 +342,7 @@
     )
     kv_all = blocks_out(at, kv_pre)
     far_pre = query_all[2:3] + kv_all[2:3]
-    grad_slices, far = slices_out(at, whole_grads, kv_pre, *far_pre)
+    grad_slices, far = slices_of(at, tie(whole_grads, local_qg), False, kv_pre, *far_pre)
 
     weights = (w_query, w_key, w_value)
 
@@ -376,10 +363,8 @@
     total = None
     for k in range(1, at.Z + 1):
         held = halves(mine[k - 1])
-        due = [f for i, f in enumerate(far) if i * at.Z // len(far) + 2 == k]
-        due = due + far_pre if k == 1 else due
-        if due:
-            held = lax.optimization_barrier((*held, *due))[:2]
+        if k == min(2, at.Z):
+            held = lax.optimization_barrier((*held, *far_pre))[:2]
         if sides is not None:
             held = [h + s for h, s in zip(held, halves(sides[k - 1]))]
         if total is not None:

time: 263 us -> 250 us (0.951)
  local copies, waits for them, and re-layouts: 32.9 us -> 25.7 us
  starting transfers between devices: 47.3 us -> 43.7 us
    ppermute x23 -> x21, starting transfers between devices: 17.2 us -> 10.7 us  [across(): return lax.ppermute(x, 'ctx', [(i, i ^ j) for i in range(self.nc)])]
    ppermute x23 -> x21, waiting for transfers between devices: 35.6 us -> 29.2 us  [across(): return lax.ppermute(x, 'ctx', [(i, i ^ j) for i in range(self.nc)])]
    ppermute x15, waiting for transfers between devices: 44.1 us -> 49.5 us  [along_z(): lax.ppermute(x, 'head', [(i, (i + self.Y) % self.nh) for i in range(self....]
    unnamed x32 -> x28, local copies, waits for them, and re-layouts: 7.08 us -> 2.37 us
    slice x3 -> x2, local copies, waits for them, and re-layouts: 4.34 us -> 1.53 us  [the longest x1 0.83 us: local(): grads_a = gather_piece(at, out_grad[:cut], True, most_lin)]
  transfers between devices with their start and end apart: 53 -> 50, of which waited for: 25 -> 21; matrix products, arithmetic and copies ran while one was open for 23% -> 22% of each run, Pallas kernels for 7% -> 8%
where the time goes in v4:
time: 250 us; the launch traced here: 249 us
  waiting for transfers between devices  121 us (48%)
  starting transfers between devices  43.7 us (17%)
  matrix products  35.2 us (14%)
  local copies, waits for them, and re-layouts  25.7 us (10%)
  Pallas kernels  19.6 us (8%)
  other arithmetic  3.14 us (1%)
    ppermute x15, waiting for transfers between devices, along_z(): lax.ppermute(x, 'head', [(i, (i + self.Y) % self.nh) for i in range(self....  49.5 us
    ppermute x13, waiting for transfers between devices, along_y(): lax.ppermute(x, 'head', [(i, i // Y * Y + (i + 1) % Y) for i in range(sel...  41.9 us
    ppermute x21, waiting for transfers between devices, across(): return lax.ppermute(x, 'ctx', [(i, i ^ j) for i in range(self.nc)])  29.2 us
    ppermute x13, starting transfers between devices, along_y(): lax.ppermute(x, 'head', [(i, i // Y * Y + (i + 1) % Y) for i in range(sel...  16.5 us
    dot_general x4, matrix products, contract(): jnp.einsum('td,ti->di', left, right, preferred_element_type=F32)  16.4 us
    pallas_call x2, Pallas kernels, parts_of(): pl.pallas_call(functools.partial(part_kernel, count), out_shape=[jax.Shap...  16.1 us
    ppermute x15, starting transfers between devices, along_z(): lax.ppermute(x, 'head', [(i, (i + self.Y) % self.nh) for i in range(self....  14.9 us
    dynamic_update_slice x22, local copies, waits for them, and re-layouts, place(): whole = lax.dynamic_update_slice(whole, part, (row, where * cols))  10.8 us
  transfers between devices with their start and end apart: 50, of which 21 were waited for; matrix products, arithmetic and copies ran while one was open for 22% of the time, Pallas kernels for 8%

profile of v4, /device:TPU:0, one launch (start us, length us, event | category | flops | bytes accessed | tf_op | source)
XLA Modules:
  0.0 249.2 jit_solution(16088512728138386300)
XLA Ops:
  4.1 3.0 %collective-permute-start.1 = (bf16[160,1024]{1,0:T(8,128)(2,1)S(1)}, bf16[160,1024]{1,0:T(8,128)(2,1)S(1)}, u32[]{:S(2)}, u32[]{:S(2)}) collective-permute-start(bf16[160,1024]{1,0:T(8,128)(2,1)S(1)} %get-tuple-element.118), channel_id=1, source_target_pairs={{0,2},{1,3},{2,4},{3,5},{4,6},{5,7},{6,0},{7,1},{8,10},{9,11},{10,... | collective-permute-start | bytes 983048 | tf_op jit(solution)/shard_map/ppermute | solution.py:31
  11.3 6.4 %collective-permute-done.1 = bf16[160,1024]{1,0:T(8,128)(2,1)S(1)} collective-permute-done((bf16[160,1024]{1,0:T(8,128)(2,1)S(1)}, bf16[160,1024]{1,0:T(8,128)(2,1)S(1)}, u32[]{:S(2)}, u32[]{:S(2)}) %collective-permute-start.1) | collective-permute-done | bytes 327712 | tf_op jit(solution)/shard_map/ppermute | solution.py:31
  21.0 7.9 %collective-permute-done.9 = bf16[256,1024]{1,0:T(8,128)(2,1)S(1)} collective-permute-done((bf16[256,1024]{1,0:T(8,128)(2,1)S(1)}, bf16[256,1024]{1,0:T(8,128)(2,1)S(1)}, u32[]{:S(2)}, u32[]{:S(2)}) %collective-permute-start.9) | collective-permute-done | bytes 524320 | tf_op jit(solution)/shard_map/ppermute | solution.py:31
  30.7 5.2 %collective-permute-done.3 = bf16[160,1024]{1,0:T(8,128)(2,1)S(1)} collective-permute-done((bf16[160,1024]{1,0:T(8,128)(2,1)S(1)}, bf16[160,1024]{1,0:T(8,128)(2,1)S(1)}, u32[]{:S(2)}, u32[]{:S(2)}) %collective-permute-start.3) | collective-permute-done | bytes 327712 | tf_op jit(solution)/shard_map/ppermute | solution.py:31
  39.4 13.4 %collective-permute-done.4 = bf16[160,1024]{1,0:T(8,128)(2,1)S(1)} collective-permute-done((bf16[160,1024]{1,0:T(8,128)(2,1)S(1)}, bf16[160,1024]{1,0:T(8,128)(2,1)S(1)}, u32[]{:S(2)}, u32[]{:S(2)}) %collective-permute-start.4) | collective-permute-done | bytes 327712 | tf_op jit(solution)/shard_map/ppermute | solution.py:35
  58.0 4.1 %collective-permute-done.5 = bf16[96,1024]{1,0:T(8,128)(2,1)S(1)} collective-permute-done((bf16[96,1024]{1,0:T(8,128)(2,1)S(1)}, bf16[96,1024]{1,0:T(8,128)(2,1)S(1)}, u32[]{:S(2)}, u32[]{:S(2)}) %collective-permute-start.5) | collective-permute-done | bytes 196640 | tf_op jit(solution)/shard_map/ppermute | solution.py:35
  64.5 6.4 %collective-permute-done.12 = bf16[256,1024]{1,0:T(8,128)(2,1)S(1)} collective-permute-done((bf16[256,1024]{1,0:T(8,128)(2,1)S(1)}, bf16[256,1024]{1,0:T(8,128)(2,1)S(1)}, u32[]{:S(2)}, u32[]{:S(2)}) %collective-permute-start.12) | collective-permute-done | bytes 524320 | tf_op jit(solution)/shard_map/ppermute | solution.py:35
  84.6 6.9 %collective-permute-done.7 = bf16[96,2048]{1,0:T(8,128)(2,1)S(1)} collective-permute-done((bf16[96,2048]{1,0:T(8,128)(2,1)S(1)}, bf16[96,2048]{1,0:T(8,128)(2,1)S(1)}, u32[]{:S(2)}, u32[]{:S(2)}) %collective-permute-start.7) | collective-permute-done | bytes 393248 | tf_op jit(solution)/shard_map/ppermute | solution.py:31
  99.7 7.0 %fusion.49.ga_ref = f32[256,512]{1,0:T(8,128)S(1)} fusion(bf16[256,8192]{1,0:T(8,128)(2,1)} %slice_dynamic-update-slice_fusion.2, bf16[8192,512]{1,0:T(8,128)(2,1)} %param.11), kind=kOutput, calls=%fused_computation.109 | convolution fusion | flops 2147483648 | bytes 13107200 | tf_op jit(solution)/shard_map/dot_general | solution.py:313
  111.2 23.0 %collective-permute-done.21.refs_2_ = bf16[512,128]{1,0:T(8,128)(2,1)S(1)} collective-permute-done((bf16[512,128]{1,0:T(8,128)(2,1)S(1)}, bf16[512,128]{1,0:T(8,128)(2,1)S(1)}, u32[]{:S(2)}, u32[]{:S(2)}) %collective-permute-start.21) | collective-permute-done | bytes 131104 | tf_op jit(solution)/shard_map/ppermute | solution.py:42
  136.0 2.6 %fusion.11.gb_ref = f32[256,512]{1,0:T(8,128)S(1)} fusion(bf16[8192,512]{1,0:T(8,128)(2,1)} %param.11, s32[]{:T(128)S(6)} %select_n.256, bf16[256,8192]{1,0:T(8,128)(2,1)} %slice_dynamic-update-slice_fusion), kind=kOutput, calls=%fused_computation.14 | convolution fusion | flops 536870912 | bytes 3671040 | tf_op jit(solution)/shard_map/dot_general | solution.py:282
  141.3 3.5 %constant_dynamic-slice_fusion.1 = (bf16[256,2048]{1,0:T(8,128)(2,1)S(1)}, bf16[256,2048]{1,0:T(8,128)(2,1)}, bf16[1,256,2048]{2,1,0:T(8,128)(2,1)S(1)}, bf16[1,256,2048]{2,1,0:T(8,128)(2,1)S(1)}) fusion(bf16[256,8192]{1,0:T(8,128)(2,1)} %slice_dynamic-update-slice_fusion, s32[]{:T(128)S(6)} %select_n.261, s32[]{:T(128)S(6)} %select_n.262, ...), kind=kLoop, calls=%fused_computation.72 | loop fusion | bytes 8388624 | tf_op jit(solution)/shard_map/dynamic_slice | solution.py:88
  148.9 8.1 %shard_map.107 = (bf16[1024,256]{1,0:T(8,128)(2,1)S(1)}, bf16[1024,256]{1,0:T(8,128)(2,1)S(1)}, bf16[1024,256]{1,0:T(8,128)(2,1)S(1)}, bf16[1024,256]{1,0:T(8,128)(2,1)S(1)}) custom-call(s32[4]{0:T(128)S(1)} %get-tuple-element.121.s_ref, bf16[512,256]{1,0:T(8,128)(2,1)S(1)} %get-tuple-element.64.q_ref, bf16[2,512,256]{2,1,0:T(8,128)(2,1)S(1)} %get-tuple-element.69.kv_ref, ...), custom_call_target="tpu_custom_call" | custom-call | flops 1000 | bytes 1000 | tf_op jit(solution)/shard_map/pallas_call | solution.py:246
  163.6 8.1 %shard_map.106 = (f32[1024,256]{1,0:T(8,128)S(1)}, f32[1024,256]{1,0:T(8,128)S(1)}, f32[1024,256]{1,0:T(8,128)S(1)}, f32[1024,256]{1,0:T(8,128)S(1)}) custom-call(s32[4]{0:T(128)S(1)} %get-tuple-element.120.s_ref, bf16[512,256]{1,0:T(8,128)(2,1)S(1)} %get-tuple-element.64.q_ref, bf16[2,512,256]{2,1,0:T(8,128)(2,1)S(1)} %get-tuple-element.69.kv_ref, ...), custom_call_target="tpu_custom_call" | custom-call | flops 1000 | bytes 1000 | tf_op jit(solution)/shard_map/pallas_call | solution.py:246
  175.6 6.6 %collective-permute-done.29 = bf16[1024,256]{1,0:T(8,128)(2,1)S(1)} collective-permute-done((bf16[1024,256]{1,0:T(8,128)(2,1)S(1)}, bf16[1024,256]{1,0:T(8,128)(2,1)S(1)}, u32[]{:S(2)}, u32[]{:S(2)}) %collective-permute-start.29) | collective-permute-done | bytes 524320 | tf_op jit(solution)/shard_map/ppermute | solution.py:35
  189.8 8.2 %collective-permute-done.26 = bf16[1024,256]{1,0:T(8,128)(2,1)S(1)} collective-permute-done((bf16[1024,256]{1,0:T(8,128)(2,1)S(1)}, bf16[1024,256]{1,0:T(8,128)(2,1)S(1)}, u32[]{:S(2)}, u32[]{:S(2)}) %collective-permute-start.26) | collective-permute-done | bytes 524320 | tf_op jit(solution)/shard_map/ppermute | solution.py:35
  200.7 5.4 %collective-permute-done.35 = bf16[512,256]{1,0:T(8,128)(2,1)S(1)} collective-permute-done((bf16[512,256]{1,0:T(8,128)(2,1)S(1)}, bf16[512,256]{1,0:T(8,128)(2,1)S(1)}, u32[]{:S(2)}, u32[]{:S(2)}) %collective-permute-start.35) | collective-permute-done | bytes 262176 | tf_op jit(solution)/shard_map/ppermute | solution.py:31
  210.6 8.3 %collective-permute-done.33 = bf16[512,256]{1,0:T(8,128)(2,1)S(1)} collective-permute-done((bf16[512,256]{1,0:T(8,128)(2,1)S(1)}, bf16[512,256]{1,0:T(8,128)(2,1)S(1)}, u32[]{:S(2)}, u32[]{:S(2)}) %collective-permute-start.33) | collective-permute-done | bytes 262176 | tf_op jit(solution)/shard_map/ppermute | solution.py:31
  218.8 3.7 %collective-permute-done.36 = bf16[512,256]{1,0:T(8,128)(2,1)S(1)} collective-permute-done((bf16[512,256]{1,0:T(8,128)(2,1)S(1)}, bf16[512,256]{1,0:T(8,128)(2,1)S(1)}, u32[]{:S(2)}, u32[]{:S(2)}) %collective-permute-start.36) | collective-permute-done | bytes 262176 | tf_op jit(solution)/shard_map/ppermute | solution.py:31
  224.9 3.7 %convolution_convert_fusion.2 = bf16[2048,512]{1,0:T(8,128)(2,1)} fusion(bf16[1024,2048]{1,0:T(8,128)(2,1)S(1)} %pad_maximum_fusion, bf16[256,512]{1,0:T(8,128)(2,1)S(1)} %collective-permute-done.42, bf16[256,512]{1,0:T(8,128)(2,1)S(1)} %collective-permute-done.27, bf16[256,512]{1,0:T(8,128)(2,1)S(1)} %collective-permute-done.41, ...), kind=kOutput, calls=%fused_computation.12 | convolution fusion | flops 2152726528 | bytes 7340032 | tf_op jit(solution)/shard_map/td,ti->di/dot_general | solution.py:381
  228.6 5.7 %collective-permute-done.37 = bf16[2,256,2048]{2,1,0:T(8,128)(2,1)S(1)} collective-permute-done((bf16[2,256,2048]{2,1,0:T(8,128)(2,1)S(1)}, bf16[2,256,2048]{2,1,0:T(8,128)(2,1)S(1)}, u32[]{:S(2)}, u32[]{:S(2)}) %collective-permute-start.37) | collective-permute-done | bytes 2097184 | tf_op jit(solution)/shard_map/ppermute | solution.py:42
  235.4 3.7 %convolution_convert_fusion = bf16[2048,512]{1,0:T(8,128)(2,1)} fusion(bf16[1024,2048]{1,0:T(8,128)(2,1)S(1)} %pad_maximum_fusion, bf16[2,1024,512]{2,1,0:T(8,128)(2,1)S(1)} %constant_dynamic-update-slice_fusion), kind=kOutput, calls=%fused_computation.10 | convolution fusion | flops 2148532224 | bytes 7340032 | tf_op jit(solution)/shard_map/td,ti->di/dot_general | solution.py:381
  239.1 3.7 %convolution_convert_fusion.1 = bf16[2048,512]{1,0:T(8,128)(2,1)} fusion(bf16[1024,2048]{1,0:T(8,128)(2,1)S(1)} %pad_maximum_fusion, bf16[2,1024,512]{2,1,0:T(8,128)(2,1)S(1)} %constant_dynamic-update-slice_fusion), kind=kOutput, calls=%fused_computation.11 | convolution fusion | flops 2148532224 | bytes 7340032 | tf_op jit(solution)/shard_map/td,ti->di/dot_general | solution.py:381
  243.9 5.3 %fusion.8 = bf16[2048,512]{1,0:T(8,128)(2,1)} fusion(bf16[256,2048]{1,0:T(8,128)(2,1)} %collective-permute-done.46, bf16[256,2048]{1,0:T(8,128)(2,1)S(1)} %get-tuple-element.102, bf16[256,2048]{1,0:T(8,128)(2,1)} %collective-permute-done.45, bf16[256,2048]{1,0:T(8,128)(2,1)S(1)} %get-tuple-element.94, bf16[256,512]{1,0:T(8,128)(2,1)} %collective-permute-done.49, ...), kind=kOutput, calls=%fused_computation.9 | convolution fusion | flops 2169503744 | bytes 7340032 | tf_op jit(solution)/shard_map/td,ti->di/dot_general | solution.py:381
  (173 shorter events, 87.9 us)
Async XLA Ops:
  8.6 20.3 %collective-permute-start.9 = (bf16[256,1024]{1,0:T(8,128)(2,1)S(1)}, bf16[256,1024]{1,0:T(8,128)(2,1)S(1)}, u32[]{:S(2)}, u32[]{:S(2)}) collective-permute-start(bf16[256,1024]{1,0:T(8,128)(2,1)S(1)} %copy-done.3), channel_id=1, source_target_pairs={{0,2},{1,3},{2,4},{3,5},{4,6},{5,7},{6,0},{7,1},{8,10},{9,11},{10,... | collective-permute-start | bytes 1572872 | tf_op jit(solution)/shard_map/ppermute | solution.py:31
  10.2 20.5 %collective-permute-start.8 = (bf16[256,1024]{1,0:T(8,128)(2,1)S(1)}, bf16[256,1024]{1,0:T(8,128)(2,1)S(1)}, u32[]{:S(2)}, u32[]{:S(2)}) collective-permute-start(bf16[256,1024]{1,0:T(8,128)(2,1)S(1)} %copy-done.3), channel_id=1, source_target_pairs={{0,1},{1,0},{2,3},{3,2},{4,5},{5,4},{6,7},{7,6},{8,9},{9,8},{10,11... | collective-permute-start | bytes 1572872 | tf_op jit(solution)/shard_map/ppermute | solution.py:35
  17.7 20.1 %collective-permute-start.2 = (bf16[160,1024]{1,0:T(8,128)(2,1)S(1)}, bf16[160,1024]{1,0:T(8,128)(2,1)S(1)}, u32[]{:S(2)}, u32[]{:S(2)}) collective-permute-start(bf16[160,1024]{1,0:T(8,128)(2,1)S(1)} %collective-permute-done.1), channel_id=1, source_target_pairs={{0,1},{1,0},{2,3},{3,2},{4,5},{5,4},{6,7},{7,6},{8,9},{9,8},{10,11... | collective-permute-start | bytes 983048 | tf_op jit(solution)/shard_map/ppermute | solution.py:35
  28.9 29.0 %collective-permute-start.10 = (bf16[256,1024]{1,0:T(8,128)(2,1)S(1)}, bf16[256,1024]{1,0:T(8,128)(2,1)S(1)}, u32[]{:S(2)}, u32[]{:S(2)}) collective-permute-start(bf16[256,1024]{1,0:T(8,128)(2,1)S(1)} %collective-permute-done.9), channel_id=1, source_target_pairs={{0,1},{1,0},{2,3},{3,2},{4,5},{5,4},{6,7},{7,6},{8,9},{9,8},{10,11... | collective-permute-start | bytes 1572872 | tf_op jit(solution)/shard_map/ppermute | solution.py:35
  30.6 25.2 %collective-permute-start.11 = (bf16[256,1024]{1,0:T(8,128)(2,1)S(1)}, bf16[256,1024]{1,0:T(8,128)(2,1)S(1)}, u32[]{:S(2)}, u32[]{:S(2)}) collective-permute-start(bf16[256,1024]{1,0:T(8,128)(2,1)S(1)} %collective-permute-done.9), channel_id=1, source_target_pairs={{0,2},{1,3},{2,4},{3,5},{4,6},{5,7},{6,0},{7,1},{8,10},{9,11},{10,... | collective-permute-start | bytes 1572872 | tf_op jit(solution)/shard_map/ppermute | solution.py:31
  35.9 16.9 %collective-permute-start.4 = (bf16[160,1024]{1,0:T(8,128)(2,1)S(1)}, bf16[160,1024]{1,0:T(8,128)(2,1)S(1)}, u32[]{:S(2)}, u32[]{:S(2)}) collective-permute-start(bf16[160,1024]{1,0:T(8,128)(2,1)S(1)} %collective-permute-done.3), channel_id=1, source_target_pairs={{0,1},{1,0},{2,3},{3,2},{4,5},{5,4},{6,7},{7,6},{8,9},{9,8},{10,11... | collective-permute-start | bytes 983048 | tf_op jit(solution)/shard_map/ppermute | solution.py:35
  37.7 43.3 %collective-permute-start.16 = (bf16[160,1024]{1,0:T(8,128)(2,1)S(1)}, bf16[160,1024]{1,0:T(8,128)(2,1)S(1)}, u32[]{:S(2)}, u32[]{:S(2)}) collective-permute-start(bf16[160,1024]{1,0:T(8,128)(2,1)S(1)} %collective-permute-done.3), channel_id=1, source_target_pairs={{0,2},{1,3},{2,4},{3,5},{4,6},{5,7},{6,0},{7,1},{8,10},{9,11},{10,... | collective-permute-start | bytes 983048 | tf_op jit(solution)/shard_map/ppermute | solution.py:31
  56.3 23.1 %collective-permute-start.13 = (bf16[256,1024]{1,0:T(8,128)(2,1)S(1)}, bf16[256,1024]{1,0:T(8,128)(2,1)S(1)}, u32[]{:S(2)}, u32[]{:S(2)}) collective-permute-start(bf16[256,1024]{1,0:T(8,128)(2,1)S(1)} %collective-permute-done.11), channel_id=1, source_target_pairs={{0,2},{1,3},{2,4},{3,5},{4,6},{5,7},{6,0},{7,1},{8,10},{9,11},{10,... | collective-permute-start | bytes 1572872 | tf_op jit(solution)/shard_map/ppermute | solution.py:31
  62.1 19.4 %collective-permute-start.6 = (bf16[96,2048]{1,0:T(8,128)(2,1)S(1)}, bf16[96,2048]{1,0:T(8,128)(2,1)S(1)}, u32[]{:S(2)}, u32[]{:S(2)}) collective-permute-start(bf16[96,2048]{1,0:T(8,128)(2,1)S(1)} %pad_maximum_fusion.3), channel_id=1, source_target_pairs={{0,2},{1,3},{2,4},{3,5},{4,6},{5,7},{6,0},{7,1},{8,10},{9,11},{10,... | collective-permute-start | bytes 1179656 | tf_op jit(solution)/shard_map/ppermute | solution.py:31
  81.0 27.7 %collective-permute-start.17 = (bf16[160,1024]{1,0:T(8,128)(2,1)S(1)}, bf16[160,1024]{1,0:T(8,128)(2,1)S(1)}, u32[]{:S(2)}, u32[]{:S(2)}) collective-permute-start(bf16[160,1024]{1,0:T(8,128)(2,1)S(1)} %collective-permute-done.16), channel_id=1, source_target_pairs={{0,1},{1,0},{2,3},{3,2},{4,5},{5,4},{6,7},{7,6},{8,9},{9,8},{10,11... | collective-permute-start | bytes 983048 | tf_op jit(solution)/shard_map/ppermute | solution.py:35
  91.5 43.1 %collective-permute-start.18 = (bf16[96,2048]{1,0:T(8,128)(2,1)S(1)}, bf16[96,2048]{1,0:T(8,128)(2,1)S(1)}, u32[]{:S(2)}, u32[]{:S(2)}) collective-permute-start(bf16[96,2048]{1,0:T(8,128)(2,1)S(1)} %collective-permute-done.7), channel_id=1, source_target_pairs={{0,2},{1,3},{2,4},{3,5},{4,6},{5,7},{6,0},{7,1},{8,10},{9,11},{10,... | collective-permute-start | bytes 1179656 | tf_op jit(solution)/shard_map/ppermute | solution.py:31
  106.9 31.8 %collective-permute-start.15 = (bf16[2,128,2048]{2,1,0:T(8,128)(2,1)S(1)}, bf16[2,128,2048]{2,1,0:T(8,128)(2,1)}, u32[]{:S(2)}, u32[]{:S(2)}) collective-permute-start(bf16[2,128,2048]{2,1,0:T(8,128)(2,1)S(1)} %pad_maximum_fusion.2), channel_id=1, source_target_pairs={{0,16},{8,24},{16,0},{24,8},{1,17},{9,25},{17,1},{25,9},{2,18},{10... | collective-permute-start | bytes 3145736 | tf_op jit(solution)/shard_map/ppermute | solution.py:42
  108.6 25.6 %collective-permute-start.21 = (bf16[512,128]{1,0:T(8,128)(2,1)S(1)}, bf16[512,128]{1,0:T(8,128)(2,1)S(1)}, u32[]{:S(2)}, u32[]{:S(2)}) collective-permute-start(bf16[512,128]{1,0:T(8,128)(2,1)S(1)} %get-tuple-element.48), channel_id=1, source_target_pairs={{0,24},{8,16},{16,8},{24,0},{1,25},{9,17},{17,9},{25,1},{2,26},{10... | collective-permute-start | bytes 393224 | tf_op jit(solution)/shard_map/ppermute | solution.py:42
  146.1 26.4 %collective-permute-start.27 = (bf16[256,512]{1,0:T(8,128)(2,1)S(1)}, bf16[256,512]{1,0:T(8,128)(2,1)S(1)}, u32[]{:S(2)}, u32[]{:S(2)}) collective-permute-start(bf16[256,512]{1,0:T(8,128)(2,1)S(1)} %get-tuple-element.75), channel_id=1, source_target_pairs={{0,16},{8,24},{16,0},{24,8},{1,17},{9,25},{17,1},{25,9},{2,18},{10... | collective-permute-start | bytes 786440 | tf_op jit(solution)/shard_map/ppermute | solution.py:42
  146.8 41.9 %collective-permute-start.39 = (bf16[2,128,2048]{2,1,0:T(8,128)(2,1)}, bf16[2,128,2048]{2,1,0:T(8,128)(2,1)S(1)}, u32[]{:S(2)}, u32[]{:S(2)}) collective-permute-start(bf16[2,128,2048]{2,1,0:T(8,128)(2,1)} %collective-permute-done.15), channel_id=1, source_target_pairs={{0,2},{1,3},{2,0},{3,1},{4,6},{5,7},{6,4},{7,5},{8,10},{9,11},{10,... | collective-permute-start | bytes 3145736 | tf_op jit(solution)/shard_map/ppermute | solution.py:39
  161.5 20.7 %collective-permute-start.29 = (bf16[1024,256]{1,0:T(8,128)(2,1)S(1)}, bf16[1024,256]{1,0:T(8,128)(2,1)S(1)}, u32[]{:S(2)}, u32[]{:S(2)}) collective-permute-start(bf16[1024,256]{1,0:T(8,128)(2,1)S(1)} %get-tuple-element.78), channel_id=1, source_target_pairs={{0,1},{1,0},{2,3},{3,2},{4,5},{5,4},{6,7},{7,6},{8,9},{9,8},{10,11... | collective-permute-start | bytes 1572872 | tf_op jit(solution)/shard_map/ppermute | solution.py:35
  186.9 20.9 %collective-permute-start.25 = (bf16[1024,256]{1,0:T(8,128)(2,1)S(1)}, bf16[1024,256]{1,0:T(8,128)(2,1)S(1)}, u32[]{:S(2)}, u32[]{:S(2)}) collective-permute-start(bf16[1024,256]{1,0:T(8,128)(2,1)S(1)} %get-tuple-element.71), channel_id=1, source_target_pairs={{0,1},{1,0},{2,3},{3,2},{4,5},{5,4},{6,7},{7,6},{8,9},{9,8},{10,11... | collective-permute-start | bytes 1572872 | tf_op jit(solution)/shard_map/ppermute | solution.py:35
  188.7 45.6 %collective-permute-start.37 = (bf16[2,256,2048]{2,1,0:T(8,128)(2,1)S(1)}, bf16[2,256,2048]{2,1,0:T(8,128)(2,1)S(1)}, u32[]{:S(2)}, u32[]{:S(2)}) collective-permute-start(bf16[2,256,2048]{2,1,0:T(8,128)(2,1)S(1)} %copy-done), channel_id=1, source_target_pairs={{0,16},{8,24},{16,0},{24,8},{1,17},{9,25},{17,1},{25,9},{2,18},{10... | collective-permute-start | bytes 6291464 | tf_op jit(solution)/shard_map/ppermute | solution.py:42
  189.6 19.2 %collective-permute-start.44 = (bf16[2,256,512]{2,1,0:T(8,128)(2,1)S(1)}, bf16[2,256,512]{2,1,0:T(8,128)(2,1)S(1)}, u32[]{:S(2)}, u32[]{:S(2)}) collective-permute-start(bf16[2,256,512]{2,1,0:T(8,128)(2,1)S(1)} %collective-permute-done.28), channel_id=1, source_target_pairs={{0,8},{8,0},{16,24},{24,16},{1,9},{9,1},{17,25},{25,17},{2,10},{10... | collective-permute-start | bytes 1572872 | tf_op jit(solution)/shard_map/ppermute | solution.py:42
  200.7 22.1 %collective-permute-start.38 = (bf16[256,2048]{1,0:T(8,128)(2,1)S(1)}, bf16[256,2048]{1,0:T(8,128)(2,1)S(1)}, u32[]{:S(2)}, u32[]{:S(2)}) collective-permute-start(bf16[256,2048]{1,0:T(8,128)(2,1)S(1)} %copy-done.1), channel_id=1, source_target_pairs={{0,8},{8,0},{16,24},{24,16},{1,9},{9,1},{17,25},{25,17},{2,10},{10... | collective-permute-start | bytes 3145736 | tf_op jit(solution)/shard_map/ppermute | solution.py:42
  206.1 17.3 %collective-permute-start.40 = (bf16[256,2048]{1,0:T(8,128)(2,1)S(1)}, bf16[256,2048]{1,0:T(8,128)(2,1)S(1)}, u32[]{:S(2)}, u32[]{:S(2)}) collective-permute-start(bf16[256,2048]{1,0:T(8,128)(2,1)S(1)} %get-tuple-element.105), channel_id=1, source_target_pairs={{0,8},{8,0},{16,24},{24,16},{1,9},{9,1},{17,25},{25,17},{2,10},{10... | collective-permute-start | bytes 3145736 | tf_op jit(solution)/shard_map/ppermute | solution.py:42
  218.8 25.1 %collective-permute-start.47 = (bf16[256,512]{1,0:T(8,128)(2,1)S(1)}, bf16[256,512]{1,0:T(8,128)(2,1)S(1)}, u32[]{:S(2)}, u32[]{:S(2)}) collective-permute-start(bf16[256,512]{1,0:T(8,128)(2,1)S(1)} %get-tuple-element.88), channel_id=1, source_target_pairs={{0,8},{8,0},{16,24},{24,16},{1,9},{9,1},{17,25},{25,17},{2,10},{10... | collective-permute-start | bytes 786440 | tf_op jit(solution)/shard_map/ppermute | solution.py:42
  222.6 21.3 %collective-permute-start.49 = (bf16[256,512]{1,0:T(8,128)(2,1)S(1)}, bf16[256,512]{1,0:T(8,128)(2,1)}, u32[]{:S(2)}, u32[]{:S(2)}) collective-permute-start(bf16[256,512]{1,0:T(8,128)(2,1)S(1)} %collective-permute-done.48), channel_id=1, source_target_pairs={{0,8},{8,0},{16,24},{24,16},{1,9},{9,1},{17,25},{25,17},{2,10},{10... | collective-permute-start | bytes 786440 | tf_op jit(solution)/shard_map/ppermute | solution.py:42
  224.6 19.3 %collective-permute-start.45 = (bf16[256,2048]{1,0:T(8,128)(2,1)}, bf16[256,2048]{1,0:T(8,128)(2,1)}, u32[]{:S(2)}, u32[]{:S(2)}) collective-permute-start(bf16[256,2048]{1,0:T(8,128)(2,1)} %get-tuple-element.87), channel_id=1, source_target_pairs={{0,8},{8,0},{16,24},{24,16},{1,9},{9,1},{17,25},{25,17},{2,10},{10... | collective-permute-start | bytes 3145736 | tf_op jit(solution)/shard_map/ppermute | solution.py:42
  (38 other events, 466.4 us)
